TPU v7x, 32 devices: a whole 2x2x4 slice. The times are simulated.
32 devices in a mesh: row: 4 (over y, x), col: 8 (over z, core).
Axes of the slice: x: 2, y: 2, z: 4, core: 2. Of those that a mesh axis runs over, the one named last changes fastest.
Arguments:
- bin_features: bfloat16 [1024, 512], P('row'), may hold values from -6 to 6
- w_left: bfloat16 [512, 32], replicated, may hold values from -0.25 to 0.25
- w_right: bfloat16 [512, 32], replicated, may hold values from -0.25 to 0.25
- depth_kernel: float32 [9, 32], replicated, may hold values from -2 to 2
- w_point: bfloat16 [32, 32], replicated, may hold values from -1 to 1
- w_head: bfloat16 [32, 24], replicated, may hold values from -1 to 1
- cotangent: bfloat16 [24, 1024, 1024], P(None, 'row', 'col'), may hold values from -6 to 6
Outputs:
- grad_features: bfloat16 [1024, 512], P('row')
- grad_w_left: float32 [512, 32], replicated
- grad_w_right: float32 [512, 32], replicated
- grad_kernel: float32 [9, 32], replicated
- grad_point: float32 [32, 32], replicated
- grad_head: float32 [32, 24], replicated
All inputs are finite; a program needn't handle non-finite values.
Results may differ from a plain program's by a relative error of at most 0.019.
Values may be sent and summed in bfloat16 or wider, within the bound.
A program may use at most 64 MiB of HBM per device.

v0:
```python
import math

import jax
import jax.numpy as jnp
from jax import lax
from jax.sharding import PartitionSpec as P

DILATION_STEP = 4


def from_root(block, axis, source):
    block = jnp.where(lax.axis_index(axis) == source, block, jnp.zeros_like(block))
    return lax.psum(block, axis)


def extended(x, sides, width):
    for axis, dim in sides:
        count, length = (lax.axis_size(axis), x.shape[dim])
        up = [(i, (i + 1) % count) for i in range(count - 1)]
        down = [(j, i) for i, j in up]
        last = lax.slice_in_dim(x, length - width, length, axis=dim)
        first = lax.slice_in_dim(x, 0, width, axis=dim)
        before = lax.ppermute(last, axis, up)
        after = lax.ppermute(first, axis, down)
        x = jnp.concatenate([before, x, after], axis=dim)
    return x


def silu_slope(values):
    logistic = jax.nn.sigmoid(values)
    return logistic * (1.0 + values * (1.0 - logistic))


def depthwise(kernel_taps, padded, output_rows, output_columns):
    result = jnp.zeros((padded.shape[0], output_rows, output_columns), jnp.float32)
    for kernel_tap_row in range(3):
        for kernel_tap_column in range(3):
            result = result + kernel_taps[3 * kernel_tap_row + kernel_tap_column][
                :, None, None
            ] * padded[
                :,
                DILATION_STEP * kernel_tap_row : DILATION_STEP * kernel_tap_row + output_rows,
                DILATION_STEP * kernel_tap_column : DILATION_STEP * kernel_tap_column
                + output_columns,
            ].astype(
                jnp.float32
            )
    return result


def body(bin_features, w_left, w_right, depth_kernel, w_point, w_head, cotangent):
    rows_per_tile = bin_features.shape[0]
    columns_per_tile = cotangent.shape[2]
    chans = w_left.shape[1]
    row_count = lax.axis_size("row")
    col_count = lax.axis_size("col")
    panel_ratio = col_count // row_count
    contact_map_bins = rows_per_tile * row_count
    grad_scale = 1.0 / math.sqrt(contact_map_bins)
    row_index = lax.axis_index("row")
    col_index = lax.axis_index("col")
    left_panel = jnp.dot(bin_features, w_left, preferred_element_type=jnp.float32).astype(
        jnp.bfloat16
    )
    offset = col_index % panel_ratio * columns_per_tile
    own_rows = lax.dynamic_slice_in_dim(bin_features, offset, columns_per_tile, 0)
    right_own = jnp.dot(own_rows, w_right, preferred_element_type=jnp.float32).astype(jnp.bfloat16)
    right_panel = from_root(right_own, "row", col_index // panel_ratio)
    pair_matrix = (
        left_panel.astype(jnp.float32).T[:, :, None] + right_panel.astype(jnp.float32).T[:, None, :]
    ).astype(jnp.bfloat16)
    extended_pair = extended(pair_matrix, (("row", 1), ("col", 2)), DILATION_STEP)
    convolved_map = depthwise(depth_kernel, extended_pair, rows_per_tile, columns_per_tile)
    trunk_gradient = (
        grad_scale
        * jnp.einsum("ch,hij->cij", w_head, cotangent, preferred_element_type=jnp.float32)
    ).astype(jnp.bfloat16)
    grad_hidden = jnp.einsum(
        "co,oij->cij", w_point, trunk_gradient, preferred_element_type=jnp.float32
    )
    convolved_gradient = (grad_hidden * silu_slope(convolved_map)).astype(jnp.bfloat16)
    extended_gradient = extended(convolved_gradient, (("row", 1), ("col", 2)), DILATION_STEP)
    hidden_state = jax.nn.silu(convolved_map).astype(jnp.bfloat16)
    mixed_out = jnp.einsum("co,cij->oij", w_point, hidden_state, preferred_element_type=jnp.float32)
    centre_offset = extended_pair[
        :,
        DILATION_STEP : DILATION_STEP + rows_per_tile,
        DILATION_STEP : DILATION_STEP + columns_per_tile,
    ]
    trunk_matrix = (centre_offset.astype(jnp.float32) + mixed_out).astype(jnp.bfloat16)
    conv_f32 = convolved_gradient.astype(jnp.float32)
    backward_pass = jnp.zeros((chans, rows_per_tile, columns_per_tile), jnp.float32)
    kern_terms = []
    for kernel_tap_row in range(3):
        for kernel_tap_column in range(3):
            backward_pass = backward_pass + depth_kernel[3 * kernel_tap_row + kernel_tap_column][
                :, None, None
            ] * extended_gradient[
                :,
                DILATION_STEP * (2 - kernel_tap_row) : DILATION_STEP * (2 - kernel_tap_row)
                + rows_per_tile,
                DILATION_STEP * (2 - kernel_tap_column) : DILATION_STEP * (2 - kernel_tap_column)
                + columns_per_tile,
            ].astype(
                jnp.float32
            )
            shifted_window = extended_pair[
                :,
                DILATION_STEP * kernel_tap_row : DILATION_STEP * kernel_tap_row + rows_per_tile,
                DILATION_STEP * kernel_tap_column : DILATION_STEP * kernel_tap_column
                + columns_per_tile,
            ].astype(jnp.float32)
            kern_terms.append(jnp.sum(conv_f32 * shifted_window, axis=(1, 2)))
    kernel_part = jnp.stack(kern_terms)
    pair_gradient = trunk_gradient.astype(jnp.float32) + backward_pass
    left_part = jnp.sum(pair_gradient, axis=2).T
    right_part = jnp.sum(pair_gradient, axis=1).T
    point_part = jnp.einsum(
        "fsk,gsk->fg", hidden_state, trunk_gradient, preferred_element_type=jnp.float32
    )
    head_part = jnp.einsum(
        "ydq,gdq->yg", trunk_matrix, cotangent, preferred_element_type=jnp.float32
    )
    grad_left = lax.psum(left_part, "col").astype(jnp.bfloat16)
    column_total = lax.psum(right_part, "row").astype(jnp.bfloat16)
    all_panels = lax.all_gather(column_total, "col", axis=0, tiled=True)
    grad_right = lax.dynamic_slice_in_dim(all_panels, row_index * rows_per_tile, rows_per_tile, 0)
    grad_features = (
        jnp.dot(grad_left, w_left.T, preferred_element_type=jnp.float32)
        + jnp.dot(grad_right, w_right.T, preferred_element_type=jnp.float32)
    ).astype(jnp.bfloat16)
    contract = (((0,), (0,)), ((), ()))
    wleft_part = lax.dot_general(
        bin_features, grad_left, contract, preferred_element_type=jnp.float32
    )
    wright_part = lax.dot_general(
        bin_features, grad_right, contract, preferred_element_type=jnp.float32
    )
    kernel_sum, point_sum, head_sum = lax.psum((kernel_part, point_part, head_part), ("row", "col"))
    wleft_sum, wright_sum = lax.psum((wleft_part, wright_part), "row")
    return (
        grad_features,
        grad_scale * wleft_sum,
        grad_scale * wright_sum,
        grad_scale * kernel_sum,
        grad_scale * point_sum,
        grad_scale * head_sum,
    )


def solution(mesh):
    placed = (P("row", None), P(), P(), P(), P(), P(), P(None, "row", "col"))
    return jax.shard_map(
        body,
        mesh=mesh,
        in_specs=placed,
        out_specs=(P("row", None), P(), P(), P(), P(), P()),
        check_vma=False,
    )
```

profile of v0, /device:TPU:0, one launch (start us, length us, event | category | flops | bytes accessed | tf_op | source)
XLA Modules:
  0.0 293.2 jit_solution(7419399753090947448)
XLA Ops:
  7.3 1.1 fusion.34
  8.4 11.5 %psum.56 = bf16[32,128]{1,0:T(8,128)(2,1)S(1)} all-reduce(bf16[32,128]{1,0:T(8,128)(2,1)S(1)} %fusion.34), channel_id=1, replica_groups=mesh['row'=4,'col'=8] {'row'}, use_global_device_ids=true, to_apply=%region_0.1 | all-reduce | flops 4096 | bytes 16384 | tf_op jit(solution)/shard_map/psum | solution.py:13
  19.9 1.1 fusion.29
  21.2 1.7 add_convert_fusion
  22.9 1.5 collective-permute-start
  24.5 1.3 collective-permute-start.1
  25.8 3.5 %multiply_convert_fusion.1 = bf16[32,256,128]{2,0,1:T(8,128)(2,1)} fusion(bf16[24,256,128]{2,1,0:T(8,128)(2,1)S(1)} %copy-done, bf16[32,24]{0,1:T(8,128)(2,1)} %param.12), kind=kOutput, calls=%fused_computation.53 | convolution fusion | flops 52428800 | bytes 3671552 | tf_op jit(solution)/shard_map/ch,hij->cij/dot_general | solution.py:76
  29.3 1.4 collective-permute-done.1
  31.0 2.9 %fusion.51 = (bf16[32,264,4]{2,0,1:T(8,128)(2,1)}, bf16[32,264,4]{2,0,1:T(8,128)(2,1)}) fusion(bf16[32,264,128]{2,0,1:T(8,128)(2,1)S(1)} %pad_maximum_fusion.2), kind=kLoop, calls=%fused_computation.102 | loop fusion | bytes 270336 | tf_op jit(solution)/shard_map/slice | solution.py:21
  33.9 3.6 %copy.20 = bf16[32,264,4]{1,0,2:T(8,128)(2,1)S(1)} copy(bf16[32,264,4]{2,0,1:T(8,128)(2,1)} %get-tuple-element.35) | data formatting | bytes 135168 | tf_op jit(solution)/shard_map/slice | solution.py:21
  37.5 3.6 %copy.22 = bf16[32,264,4]{1,0,2:T(8,128)(2,1)S(1)} copy(bf16[32,264,4]{2,0,1:T(8,128)(2,1)} %get-tuple-element.36) | data formatting | bytes 135168 | tf_op jit(solution)/shard_map/slice | solution.py:22
  41.2 1.3 collective-permute-start.3
  42.5 3.2 %collective-permute-start.2 = (bf16[32,264,4]{1,0,2:T(8,128)(2,1)S(1)}, bf16[32,264,4]{1,0,2:T(8,128)(2,1)S(1)}, u32[]{:S(2)}, u32[]{:S(2)}) collective-permute-start(bf16[32,264,4]{1,0,2:T(8,128)(2,1)S(1)} %copy.20), channel_id=1, source_target_pairs={{0,1},{1,2},{2,3},{3,4},{4,5},{5,6},{6,7},{8,9},{9,10},{10,11},{11... | collective-permute-start | bytes 202760 | tf_op jit(solution)/shard_map/ppermute | solution.py:23
  45.7 0.7 collective-permute-done.2
  46.5 3.0 %copy.21 = bf16[32,264,4]{2,0,1:T(8,128)(2,1)} copy(bf16[32,264,4]{1,0,2:T(8,128)(2,1)S(1)} %collective-permute-done.2) | data formatting | bytes 135168 | tf_op jit(solution)/shard_map/ppermute | solution.py:23
  49.5 3.0 %copy.23 = bf16[32,264,4]{2,0,1:T(8,128)(2,1)} copy(bf16[32,264,4]{1,0,2:T(8,128)(2,1)S(1)} %collective-permute-done.3) | data formatting | bytes 135168 | tf_op jit(solution)/shard_map/ppermute | solution.py:24
  52.5 7.2 %maximum_maximum_fusion = (bf16[32,264,132]{2,0,1:T(8,128)(2,1)S(1)}, bf16[32,264,132]{2,0,1:T(8,128)(2,1)S(1)}) fusion(bf16[32,4,128]{2,0,1:T(8,128)(2,1)S(1)} %collective-permute-done.1, bf16[32,256,128]{2,0,1:T(8,128)(2,1)} %copy-done.1, bf16[32,4,128]{2,0,1:T(8,128)(2,1)S(1)} %collective-permute-done, bf16[32,264,4]{2,0,1:T(8,128)(2,1)} %copy.21, ...), kind=kLoop, calls=%fused_computation.20 | loop fusion | flops 17842176 | bytes 6758400 | tf_op jit(solution)/shard_map/concatenate | solution.py:25
  59.8 10.2 %multiply_convert_fusion = (bf16[32,256,128]{2,0,1:T(8,128)(2,1)}, f32[32,256,128]{2,0,1:T(8,128)}) fusion(bf16[32,264,132]{2,0,1:T(8,128)(2,1)S(1)} %get-tuple-element.34, f32[32]{0:T(128)S(1)} %get-tuple-element.48, bf16[32,4,128]{2,0,1:T(8,128)(2,1)S(1)} %collective-permute-done.1, bf16[32,256,128]{2,0,1:T(8,128)(2,1)S(1)} %copy-done.2, ...), kind=kLoop, calls=%fused_computation.50 | loop fusion | flops 36700160 | bytes 21087360 | tf_op jit(solution)/shard_map/convert_element_type | solution.py:83
  69.9 3.4 %fusion.30 = f32[32,24]{0,1:T(8,128)S(1)} fusion(bf16[24,256,128]{2,1,0:T(8,128)(2,1)S(1)} %copy-done, bf16[32,256,128]{2,0,1:T(8,128)(2,1)} %get-tuple-element.27, f32[32,128]{1,0:T(8,128)S(1)} %transpose.34, f32[32,256]{0,1:T(8,128)S(1)} %copy.19, bf16[32,32]{1,0:T(8,128)(2,1)S(1)} %copy-done.13), kind=kOutput, calls=%fused_computation.70 | convolution fusion | flops 122683392 | bytes 3724288 | tf_op jit(solution)/shard_map/ydq,gdq->yg/dot_general | solution.py:121
  73.4 3.0 %convolution_bitcast_fusion.2 = f32[32,32]{1,0:T(8,128)S(1)} fusion(bf16[32,256,128]{2,0,1:T(8,128)(2,1)} %get-tuple-element.27, bf16[32,256,128]{2,0,1:T(8,128)(2,1)} %multiply_convert_fusion.1), kind=kOutput, calls=%fused_computation.69 | convolution fusion | flops 67108864 | bytes 4198400 | tf_op jit(solution)/shard_map/fsk,gsk->fg/dot_general | solution.py:118
  76.9 13.2 %fusion.23 = (f32[32]{0:T(128)S(1)}, f32[32]{0:T(128)S(1)}, f32[32]{0:T(128)S(1)}, f32[32]{0:T(128)S(1)}, f32[32]{0:T(128)S(1)}, /*index=5*/f32[32]{0:T(128)S(1)...) fusion(bf16[32,264,132]{2,0,1:T(8,128)(2,1)} %copy-done.5, ...), kind=kOutput, calls=%fused_computation.47 | convolution fusion | flops 110100192 | bytes 23186560 | tf_op jit(solution)/shard_map/co,oij->cij/dot_general | solution.py:78
  90.1 43.8 %all-reduce = (f32[9,32]{1,0:T(8,128)S(1)}, f32[32,32]{1,0:T(8,128)S(1)}, f32[32,24]{0,1:T(8,128)S(1)}) all-reduce(f32[9,32]{1,0:T(8,128)S(1)} %stack.39, f32[32,32]{1,0:T(8,128)S(1)} %convolution_bitcast_fusion.2, f32[32,24]{0,1:T(8,128)S(1)} %fusion.30), channel_id=1, replica_groups=mesh['row'=4,'col'=8] {'row','col'}, use_global_device_ids=true, to_apply=%region_16.17 | all-reduce | flops 2080 | bytes 16640 | tf_op jit(solution)/shard_map/psum | solution.py:139
  134.0 0.6 broadcast_multiply_fusion.2
  134.6 0.8 fusion.52
  135.4 4.0 %collective-permute-start.4 = (bf16[32,4,128]{2,0,1:T(8,128)(2,1)S(1)}, bf16[32,4,128]{2,0,1:T(8,128)(2,1)S(1)}, u32[]{:S(2)}, u32[]{:S(2)}) collective-permute-start(bf16[32,4,128]{2,0,1:T(8,128)(2,1)S(1)} %get-tuple-element.37), channel_id=1, source_target_pairs={{0,8},{8,16},{16,24},{1,9},{9,17},{17,25},{2,10},{10,18},{18,26},{... | collective-permute-start | bytes 98312 | tf_op jit(solution)/shard_map/ppermute | solution.py:23
  139.4 1.5 collective-permute-start.5
  140.9 0.6 broadcast_multiply_fusion.3
  141.5 3.7 %collective-permute-done.5 = bf16[32,4,128]{2,0,1:T(8,128)(2,1)S(1)} collective-permute-done((bf16[32,4,128]{2,0,1:T(8,128)(2,1)S(1)}, bf16[32,4,128]{2,0,1:T(8,128)(2,1)S(1)}, u32[]{:S(2)}, u32[]{:S(2)}) %collective-permute-start.5) | collective-permute-done | bytes 32800 | tf_op jit(solution)/shard_map/ppermute | solution.py:24
  145.2 1.9 pad_maximum_fusion.3
  147.1 2.9 %fusion.50 = (bf16[32,264,4]{2,0,1:T(8,128)(2,1)}, bf16[32,264,4]{2,0,1:T(8,128)(2,1)}) fusion(bf16[32,264,128]{2,0,1:T(8,128)(2,1)S(1)} %pad_maximum_fusion.3), kind=kLoop, calls=%fused_computation.101 | loop fusion | bytes 270336 | tf_op jit(solution)/shard_map/slice | solution.py:22
  150.0 3.6 %copy.24 = bf16[32,264,4]{1,0,2:T(8,128)(2,1)S(1)} copy(bf16[32,264,4]{2,0,1:T(8,128)(2,1)} %get-tuple-element.31) | data formatting | bytes 135168 | tf_op jit(solution)/shard_map/slice | solution.py:22
  153.7 3.6 %copy.26 = bf16[32,264,4]{1,0,2:T(8,128)(2,1)S(1)} copy(bf16[32,264,4]{2,0,1:T(8,128)(2,1)} %get-tuple-element.32) | data formatting | bytes 135168 | tf_op jit(solution)/shard_map/slice | solution.py:21
  157.3 1.3 collective-permute-start.7
  158.6 1.3 collective-permute-start.6
  159.9 0.6 broadcast_multiply_fusion.4
  160.5 3.0 %collective-permute-done.6 = bf16[32,264,4]{1,0,2:T(8,128)(2,1)S(1)} collective-permute-done((bf16[32,264,4]{1,0,2:T(8,128)(2,1)S(1)}, bf16[32,264,4]{1,0,2:T(8,128)(2,1)S(1)}, u32[]{:S(2)}, u32[]{:S(2)}) %collective-permute-start.6) | collective-permute-done | bytes 67616 | tf_op jit(solution)/shard_map/ppermute | solution.py:24
  163.5 3.0 %copy.25 = bf16[32,264,4]{2,0,1:T(8,128)(2,1)} copy(bf16[32,264,4]{1,0,2:T(8,128)(2,1)S(1)} %collective-permute-done.6) | data formatting | bytes 135168 | tf_op jit(solution)/shard_map/ppermute | solution.py:24
  166.6 3.0 %copy.27 = bf16[32,264,4]{2,0,1:T(8,128)(2,1)} copy(bf16[32,264,4]{1,0,2:T(8,128)(2,1)S(1)} %collective-permute-done.7) | data formatting | bytes 135168 | tf_op jit(solution)/shard_map/ppermute | solution.py:23
  169.6 7.2 %pad_maximum_fusion.1 = (bf16[32,264,132]{2,0,1:T(8,128)(2,1)S(1)}, bf16[32,264,132]{2,0,1:T(8,128)(2,1)S(1)}) fusion(bf16[32,264,4]{2,0,1:T(8,128)(2,1)} %copy.25, bf16[32,4,128]{2,0,1:T(8,128)(2,1)S(1)} %collective-permute-done.5, bf16[32,256,128]{2,0,1:T(8,128)(2,1)} %get-tuple-element.50, bf16[32,4,128]{2,0,1:T(8,128)(2,1)S(1)} %collective-permute-done.4, ...), kind=kLoop, calls=%fused_computation.22 | loop fusion | flops 17842176 | bytes 6758400 | tf_op jit(solution)/shard_map/concatenate | solution.py:25
  176.9 7.2 %fusion.48 = (f32[32,128]{1,0:T(8,128)S(1)}, f32[32,256]{0,1:T(8,128)S(1)}) fusion(bf16[32,264,132]{2,0,1:T(8,128)(2,1)S(1)} %get-tuple-element.30, f32[32]{0:T(128)S(1)} %get-tuple-element.48, bf16[32,256,128]{2,0,1:T(8,128)(2,1)S(1)} %copy-done.6, bf16[32,4,128]{2,0,1:T(8,128)(2,1)S(1)} %collective-permute-done.4, f32[32]{0:T(128)S(1)} %get-tuple-element.49, ...), kind=kLoop, calls=%fused_computation.100 | loop fusion | flops 33542144 | bytes 16893056 | tf_op jit(solution)/shard_map/reduce_sum | solution.py:117
  184.2 30.3 %psum.57 = bf16[256,32]{1,0:T(8,128)(2,1)S(1)} all-reduce(f32[256,32]{1,0:T(8,128)S(1)} %bitcast.73), channel_id=1, replica_groups=mesh['row'=4,'col'=8] {'col'}, use_global_device_ids=true, to_apply=%region_2.3 | all-reduce | flops 8192 | bytes 49152 | tf_op jit(solution)/shard_map/psum | solution.py:124
  214.5 0.8 convolution_bitcast_fusion.1
  215.5 16.1 %psum.58 = bf16[128,32]{0,1:T(8,128)(2,1)S(1)} all-reduce(f32[128,32]{0,1:T(8,128)S(1)} %bitcast.74), channel_id=1, replica_groups=mesh['row'=4,'col'=8] {'row'}, use_global_device_ids=true, to_apply=%region_4.5 | all-reduce | flops 4096 | bytes 24576 | tf_op jit(solution)/shard_map/psum | solution.py:125
  231.5 12.7 %all_gather.3 = bf16[1024,32]{0,1:T(8,128)(2,1)S(1)} all-gather(bf16[128,32]{0,1:T(8,128)(2,1)S(1)} %psum.58), channel_id=1, replica_groups=mesh['row'=4,'col'=8] {'col'}, dimensions={0}, use_global_device_ids=true | all-gather | bytes 73728 | tf_op jit(solution)/shard_map/all_gather | solution.py:126
  244.2 0.8 convolution_bitcast_fusion
  245.0 1.0 fusion.28
  246.0 38.8 %all-reduce.4.cloned.1.call-done = (f32[512,32]{0,1:T(8,128)}, f32[512,32]{0,1:T(8,128)}) async-done(((f32[512,32]{0,1:T(8,128)}, f32[512,32]{0,1:T(8,128)}), (f32[512,32]{0,1:T(8,128)}, f32[512,32]{0,1:T(8,128)})) %all-reduce.4.cloned.1.call-update) | async-done | bytes 131088 | tf_op jit(solution)/shard_map/psum | solution.py:140
  284.8 1.5 broadcast_multiply_fusion
  (41 shorter events, 1.2 us)
Async XLA Ops:
  7.2 18.6 %copy-start = (bf16[24,256,128]{2,1,0:T(8,128)(2,1)S(1)}, bf16[24,256,128]{2,1,0:T(8,128)(2,1)}, u32[]{:S(2)}) copy-start(bf16[24,256,128]{2,1,0:T(8,128)(2,1)} %param.13) | copy-start | bytes 4718596
  7.2 277.6 %all-reduce.4.cloned.1.call-start = ((), (), s32[]{:S(2)}) async-start(), calls=%async_computation | async-start | bytes 262144 | tf_op jit(solution)/shard_map/psum | solution.py:140
  22.9 7.8 %copy-start.1 = (bf16[32,256,128]{2,0,1:T(8,128)(2,1)}, bf16[32,256,128]{2,0,1:T(8,128)(2,1)S(1)}, u32[]{:S(2)}) copy-start(bf16[32,256,128]{2,0,1:T(8,128)(2,1)S(1)} %add_convert_fusion) | copy-start | bytes 6291460
  22.9 6.3 %collective-permute-start = (bf16[32,4,128]{2,0,1:T(8,128)(2,1)S(1)}, bf16[32,4,128]{2,0,1:T(8,128)(2,1)S(1)}, u32[]{:S(2)}, u32[]{:S(2)}) collective-permute-start(bf16[32,4,128]{2,0,1:T(8,128)(2,1)S(1)} %get-tuple-element.39), channel_id=1, source_target_pairs={{0,8},{8,16},{16,24},{1,9},{9,17},{17,25},{2,10},{10,18},{18,26},{... | collective-permute-start | bytes 98312 | tf_op jit(solution)/shard_map/ppermute | solution.py:23
  24.5 6.2 %collective-permute-start.1 = (bf16[32,4,128]{2,0,1:T(8,128)(2,1)S(1)}, bf16[32,4,128]{2,0,1:T(8,128)(2,1)S(1)}, u32[]{:S(2)}, u32[]{:S(2)}) collective-permute-start(bf16[32,4,128]{2,0,1:T(8,128)(2,1)S(1)} %get-tuple-element.40), channel_id=1, source_target_pairs={{8,0},{16,8},{24,16},{9,1},{17,9},{25,17},{10,2},{18,10},{26,18},{... | collective-permute-start | bytes 98312 | tf_op jit(solution)/shard_map/ppermute | solution.py:24
  33.9 11.8 %copy-start.12 = (f32[9,32]{1,0:T(8,128)S(1)}, f32[9,32]{1,0:T(8,128)}, u32[]{:S(2)}) copy-start(f32[9,32]{1,0:T(8,128)} %param.10) | copy-start | bytes 3460
  41.2 8.3 %collective-permute-start.3 = (bf16[32,264,4]{1,0,2:T(8,128)(2,1)S(1)}, bf16[32,264,4]{1,0,2:T(8,128)(2,1)S(1)}, u32[]{:S(2)}, u32[]{:S(2)}) collective-permute-start(bf16[32,264,4]{1,0,2:T(8,128)(2,1)S(1)} %copy.22), channel_id=1, source_target_pairs={{1,0},{2,1},{3,2},{4,3},{5,4},{6,5},{7,6},{9,8},{10,9},{11,10},{12... | collective-permute-start | bytes 202760 | tf_op jit(solution)/shard_map/ppermute | solution.py:24
  42.5 4.0 %collective-permute-start.2 = (bf16[32,264,4]{1,0,2:T(8,128)(2,1)S(1)}, bf16[32,264,4]{1,0,2:T(8,128)(2,1)S(1)}, u32[]{:S(2)}, u32[]{:S(2)}) collective-permute-start(bf16[32,264,4]{1,0,2:T(8,128)(2,1)S(1)} %copy.20), channel_id=1, source_target_pairs={{0,1},{1,2},{2,3},{3,4},{4,5},{5,6},{6,7},{8,9},{9,10},{10,11},{11... | collective-permute-start | bytes 202760 | tf_op jit(solution)/shard_map/ppermute | solution.py:23
  52.5 7.2 %copy-start.2 = (bf16[32,256,128]{2,0,1:T(8,128)(2,1)S(1)}, bf16[32,256,128]{2,0,1:T(8,128)(2,1)}, u32[]{:S(2)}) copy-start(bf16[32,256,128]{2,0,1:T(8,128)(2,1)} %copy-done.1) | copy-start | bytes 6291460
  59.7 10.2 %copy-start.4 = (bf16[32,264,132]{2,0,1:T(8,128)(2,1)}, bf16[32,264,132]{2,0,1:T(8,128)(2,1)S(1)}, u32[]{:S(2)}) copy-start(bf16[32,264,132]{2,0,1:T(8,128)(2,1)S(1)} %get-tuple-element.33) | copy-start | bytes 6690820
  59.7 10.2 %copy-start.5 = (bf16[32,264,132]{2,0,1:T(8,128)(2,1)}, bf16[32,264,132]{2,0,1:T(8,128)(2,1)S(1)}, u32[]{:S(2)}) copy-start(bf16[32,264,132]{2,0,1:T(8,128)(2,1)S(1)} %get-tuple-element.34) | copy-start | bytes 6690820
  59.8 10.2 %copy-start.13 = (bf16[32,32]{1,0:T(8,128)(2,1)S(1)}, bf16[32,32]{1,0:T(8,128)(2,1)}, u32[]{:S(2)}) copy-start(bf16[32,32]{1,0:T(8,128)(2,1)} %param.11) | copy-start | bytes 6148
  73.4 3.1 %copy-start.3 = (bf16[32,256,128]{2,0,1:T(8,128)(2,1)S(1)}, bf16[32,256,128]{2,0,1:T(8,128)(2,1)}, u32[]{:S(2)}) copy-start(bf16[32,256,128]{2,0,1:T(8,128)(2,1)} %copy-done.1) | copy-start | bytes 6291460
  73.4 3.5 %copy-start.7 = (bf16[32,256,128]{2,0,1:T(8,128)(2,1)S(1)}, bf16[32,256,128]{2,0,1:T(8,128)(2,1)}, u32[]{:S(2)}) copy-start(bf16[32,256,128]{2,0,1:T(8,128)(2,1)} %multiply_convert_fusion.1) | copy-start | bytes 6291460
  135.4 6.2 %collective-permute-start.4 = (bf16[32,4,128]{2,0,1:T(8,128)(2,1)S(1)}, bf16[32,4,128]{2,0,1:T(8,128)(2,1)S(1)}, u32[]{:S(2)}, u32[]{:S(2)}) collective-permute-start(bf16[32,4,128]{2,0,1:T(8,128)(2,1)S(1)} %get-tuple-element.37), channel_id=1, source_target_pairs={{0,8},{8,16},{16,24},{1,9},{9,17},{17,25},{2,10},{10,18},{18,26},{... | collective-permute-start | bytes 98312 | tf_op jit(solution)/shard_map/ppermute | solution.py:23
  139.4 5.8 %collective-permute-start.5 = (bf16[32,4,128]{2,0,1:T(8,128)(2,1)S(1)}, bf16[32,4,128]{2,0,1:T(8,128)(2,1)S(1)}, u32[]{:S(2)}, u32[]{:S(2)}) collective-permute-start(bf16[32,4,128]{2,0,1:T(8,128)(2,1)S(1)} %get-tuple-element.38), channel_id=1, source_target_pairs={{8,0},{16,8},{24,16},{9,1},{17,9},{25,17},{10,2},{18,10},{26,18},{... | collective-permute-start | bytes 98312 | tf_op jit(solution)/shard_map/ppermute | solution.py:24
  157.3 9.2 %collective-permute-start.7 = (bf16[32,264,4]{1,0,2:T(8,128)(2,1)S(1)}, bf16[32,264,4]{1,0,2:T(8,128)(2,1)S(1)}, u32[]{:S(2)}, u32[]{:S(2)}) collective-permute-start(bf16[32,264,4]{1,0,2:T(8,128)(2,1)S(1)} %copy.26), channel_id=1, source_target_pairs={{0,1},{1,2},{2,3},{3,4},{4,5},{5,6},{6,7},{8,9},{9,10},{10,11},{11... | collective-permute-start | bytes 202760 | tf_op jit(solution)/shard_map/ppermute | solution.py:23
  158.6 4.9 %collective-permute-start.6 = (bf16[32,264,4]{1,0,2:T(8,128)(2,1)S(1)}, bf16[32,264,4]{1,0,2:T(8,128)(2,1)S(1)}, u32[]{:S(2)}, u32[]{:S(2)}) collective-permute-start(bf16[32,264,4]{1,0,2:T(8,128)(2,1)S(1)} %copy.24), channel_id=1, source_target_pairs={{1,0},{2,1},{3,2},{4,3},{5,4},{6,5},{7,6},{9,8},{10,9},{11,10},{12... | collective-permute-start | bytes 202760 | tf_op jit(solution)/shard_map/ppermute | solution.py:24
  169.6 7.3 %copy-start.6 = (bf16[32,256,128]{2,0,1:T(8,128)(2,1)S(1)}, bf16[32,256,128]{2,0,1:T(8,128)(2,1)}, u32[]{:S(2)}) copy-start(bf16[32,256,128]{2,0,1:T(8,128)(2,1)} %get-tuple-element.50) | copy-start | bytes 6291460
  169.6 7.3 %copy-start.8 = (bf16[32,256,128]{2,0,1:T(8,128)(2,1)S(1)}, bf16[32,256,128]{2,0,1:T(8,128)(2,1)}, u32[]{:S(2)}) copy-start(bf16[32,256,128]{2,0,1:T(8,128)(2,1)} %multiply_convert_fusion.1) | copy-start | bytes 6291460
  176.9 37.6 %copy-start.9 = (bf16[256,512]{1,0:T(8,128)(2,1)S(1)}, bf16[256,512]{1,0:T(8,128)(2,1)}, u32[]{:S(2)}) copy-start(bf16[256,512]{1,0:T(8,128)(2,1)} %param.7) | copy-start | bytes 786436
  176.9 38.4 %copy-start.10 = (bf16[512,32]{0,1:T(8,128)(2,1)S(1)}, bf16[512,32]{0,1:T(8,128)(2,1)}, u32[]{:S(2)}) copy-start(bf16[512,32]{0,1:T(8,128)(2,1)} %param.8) | copy-start | bytes 98308
  176.9 68.1 %copy-start.11 = (bf16[512,32]{0,1:T(8,128)(2,1)S(1)}, bf16[512,32]{0,1:T(8,128)(2,1)}, u32[]{:S(2)}) copy-start(bf16[512,32]{0,1:T(8,128)(2,1)} %param.9) | copy-start | bytes 98308
Sparse Core Ops, SparseCore 0:
  245.1 39.6 all-reduce.3
where the time goes:
time: 294 us; the launch traced here: 293 us
  blocking collectives  114 us (39%)
  waiting for transfers between devices  47.7 us (16%)
  other arithmetic  39 us (13%)
  local copies, waits for them, and re-layouts  34 us (12%)
  matrix products  28.2 us (10%)
  starting transfers between devices  15.5 us (5%)
  between operations  14.4 us (5%)
    psum x1, blocking collectives, body(): lax.psum((kernel_part, point_part, head_part), ('row', 'col'))  43.8 us
    psum x1, waiting for transfers between devices, body(): wleft_sum, wright_sum = lax.psum((wleft_part, wright_part), 'row')  38.8 us
    psum x1, blocking collectives, body(): grad_left = lax.psum(left_part, 'col').astype(jnp.bfloat16)  30.3 us
    concatenate x4, other arithmetic, extended(): x = jnp.concatenate([before, x, after], axis=dim)  16.6 us
    psum x1, blocking collectives, body(): column_total = lax.psum(right_part, 'row').astype(jnp.bfloat16)  16.1 us
    dot_general x1, matrix products, body(): jnp.einsum('co,oij->cij', w_point, trunk_gradient, preferred_element_type...  13.2 us
    all_gather x1, blocking collectives, body(): all_panels = lax.all_gather(column_total, 'col', axis=0, tiled=True)  12.7 us
    psum x1, blocking collectives, from_root(): return lax.psum(block, axis)  11.5 us
  transfers between devices with their start and end apart: 9, of which 5 were waited for; matrix products, arithmetic and copies ran while one was open for 4% of the time, Pallas kernels for 0%

commit v1 on v0

v1 whole, which is shorter than its diff:
```python
import functools
import math

import jax
import jax.numpy as jnp
from jax import lax
from jax.experimental import pallas as pl
from jax.experimental.pallas import tpu as pltpu
from jax.sharding import PartitionSpec as P

STEP = 4
BF = jnp.bfloat16
F32 = jnp.float32
HI = lax.Precision.HIGHEST
GR = 16


def iota(shape, dim):
    return lax.broadcasted_iota(jnp.int32, shape, dim)


def split(x):
    hi = x.astype(BF)
    return hi, (x - hi.astype(F32)).astype(BF)


def dotf(a, b, contract=((1,), (0,)), precision=None):
    return lax.dot_general(a, b, (contract, ((), ())), precision=precision, preferred_element_type=F32)


def tile_kernel(scale, lext, rext, dk, wp, wh, cot, plx, prx, small,
                qs, ns, k2, cm, es, ecol, ecx, rs, cs, gcs, hid, xs, zl, zr):
    ch, heads = wh.shape
    tr, tc = cot.shape[1:]
    groups = tr // GR
    cg, hg = ch * GR, heads * GR
    row, col = lax.axis_index("row"), lax.axis_index("col")
    row_first, row_last = row == 0, row == lax.axis_size("row") - 1
    col_first, col_last = col == 0, col == lax.axis_size("col") - 1
    taps = [[dk[3 * a + b : 3 * a + b + 1, :] for b in range(3)] for a in range(3)]

    def edge(first, last, pos, length):
        return ((pos < STEP) & first) | ((pos >= length - STEP) & last)

    l_sh = [lext[8 + STEP * (a - 1) : 8 + STEP * (a - 1) + tr, :] for a in range(3)]
    r_sh = [rext[8 + STEP * (b - 1) : 8 + STEP * (b - 1) + tc, :] for b in range(3)]
    a1 = sum(l_sh[a] * (taps[a][0] + taps[a][1] + taps[a][2]) for a in range(3))
    da0 = sum(l_sh[a] * taps[a][0] for a in range(3))
    da2 = sum(l_sh[a] * taps[a][2] for a in range(3))
    da = -jnp.where(col_first, da0, jnp.where(col_last, da2, jnp.zeros_like(da2)))
    b1 = sum(r_sh[b] * (taps[0][b] + taps[1][b] + taps[2][b]) for b in range(3))
    db0 = sum(r_sh[b] * taps[0][b] for b in range(3))
    db2 = sum(r_sh[b] * taps[2][b] for b in range(3))
    db = -jnp.where(row_first, db0, jnp.where(row_last, db2, jnp.zeros_like(db2)))
    rind = jnp.where(edge(row_first, row_last, iota((tr, 2 * ch), 0), tr), 1.0, 0.0).astype(BF)
    qs[...] = jnp.concatenate(
        [*split(0.5 * a1), *split(0.5 * da), jnp.ones((tr, 2 * ch), BF), rind], axis=1)
    b_parts = [p.astype(F32) for p in (*split(0.5 * b1), *split(0.5 * db))]
    ns[4 * ch :, :] = jnp.concatenate(b_parts, axis=1).T.astype(BF)
    ns[: 2 * ch, :] = jnp.ones((2 * ch, tc), BF)
    ns[2 * ch : 4 * ch, :] = jnp.where(
        edge(col_first, col_last, iota((2 * ch, tc), 1), tc), 1.0, 0.0).astype(BF)
    cm[...] = jnp.where(iota((cg, 8 * ch), 0) // GR == iota((cg, 8 * ch), 1) % ch, 1.0, 0.0).astype(BF)

    w2 = (0.5 * scale * dotf(wp[...], wh[...])).astype(BF)
    e_r = jnp.where(iota((cg, ch), 0) // GR == iota((cg, ch), 1), 1.0, 0.0).astype(BF)
    e_c = jnp.where(iota((heads, hg), 1) // GR == iota((heads, hg), 0), 1.0, 0.0).astype(BF)
    w2r = dotf(e_r, w2).astype(BF)
    same = iota((cg, hg), 0) % GR == iota((cg, hg), 1) % GR
    k2[...] = jnp.where(same, dotf(w2r, e_c), 0.0).astype(BF)

    jj, part = iota((tc, 4 * ch), 0), iota((tc, 4 * ch), 1) // ch
    drop = ((part == 0) & (jj < STEP) & col_first) | ((part == 2) & (jj >= tc - STEP) & col_last)
    es[0] = jnp.where(drop | (part == 3), 0.0, 1.0).astype(BF)
    es[1] = jnp.where(part == 3, 1.0, 0.0).astype(BF)
    pr, ci = iota((4 * ch, cg), 0), iota((4 * ch, cg), 1)
    mine = (pr % ch == ci // GR) & (pr // ch < 3)
    top = (pr // ch == 0) & (ci % GR < STEP) & row_first
    low = (pr // ch == 2) & (ci % GR >= GR - STEP) & row_last
    ecol[0] = jnp.where(mine & ~top, 1.0, 0.0).astype(BF)
    ecol[1] = jnp.where(mine, 1.0, 0.0).astype(BF)
    ecol[2] = jnp.where(mine & ~low, 1.0, 0.0).astype(BF)
    ecx[...] = jnp.where(
        iota((4 * ch, hg), 0) == 3 * ch + iota((4 * ch, hg), 1) // GR, 1.0, 0.0).astype(BF)
    cs[...] = jnp.zeros_like(cs)

    chunk = 128
    lane_c = iota((1, 1, 4 * ch), 2) % ch

    def group(g, carry):
        start = pl.multiple_of(g * GR, GR)
        lanes = pl.ds(pl.multiple_of(g * tc, 128), tc)
        x = cot[:, pl.ds(start, GR), :].reshape(hg, tc)
        xs[:, lanes] = x
        q = qs[pl.ds(start, GR), :]
        total = jnp.zeros((GR, 4 * ch), F32)
        for k in range(cg // chunk):
            rows = slice(k * chunk, (k + 1) * chunk)
            n = chunk // GR
            m = (cm[rows, :].reshape(n, GR, 8 * ch) * q[None]).reshape(chunk, 8 * ch)
            u = dotf(m, ns[...])
            gh = dotf(k2[rows, :], x)
            t = jnp.tanh(u)
            p = 1.0 + t
            h = u * p
            gc = (gh * (p + h - h * t)).astype(BF)
            hid[rows, lanes] = h.astype(BF)
            gcs[rows, :] = gc
            y = dotf(gc, es[0]).reshape(n, GR, 4 * ch)
            pick = iota((n, 1, 4 * ch), 0) + k * n == lane_c
            total = total + jnp.sum(jnp.where(pick, y, 0.0), axis=0)
        y = dotf(x, es[1]).reshape(heads, GR, 4 * ch)
        total = total + jnp.sum(jnp.where(iota((heads, 1, 4 * ch), 0) == lane_c, y, 0.0), axis=0)
        rs[pl.ds(start, GR), :] = total
        kind = jnp.where(g == 0, 0, jnp.where(g == groups - 1, 2, 1))
        cs[...] += dotf(ecol[kind], gcs[...]) + dotf(ecx[...], x)
        return carry

    lax.fori_loop(0, groups, group, 0)

    prod = dotf(hid[...], xs[...], ((1,), (1,)))
    prod = jnp.sum(jnp.where(same, prod, 0.0).reshape(ch, GR, hg), axis=1)
    e_h = jnp.where(iota((hg, ch), 0) // GR == iota((hg, ch), 1), 1.0, 0.0)
    hc = dotf(prod, e_h, precision=HI)
    cst = cs[...].T
    rsv = rs[...]
    pc = dotf(l_sh[1], rsv[:, 3 * ch :], ((0,), (0,)), HI) + dotf(r_sh[1], cst[:, 3 * ch :], ((0,), (0,)), HI)
    small[:ch, :] = jnp.concatenate([hc, pc, jnp.zeros((ch, 2 * ch), F32)], axis=1)
    rows_out = []
    zero_l, zero_r = jnp.zeros((tr, ch), F32), jnp.zeros((tc, ch), F32)
    for a in range(3):
        rows_out.append(jnp.sum(jnp.concatenate([l_sh[a]] * 3 + [zero_l], axis=1) * rsv, axis=0, keepdims=True))
    for b in range(3):
        rows_out.append(jnp.sum(jnp.concatenate([r_sh[b]] * 3 + [zero_r], axis=1) * cst, axis=0, keepdims=True))
    small[ch:, :] = jnp.concatenate(rows_out + [jnp.zeros((2, 4 * ch), F32)], axis=0)

    eye = iota((ch, ch), 0) == iota((ch, ch), 1)
    whs = scale * dotf(jnp.where(iota((ch, heads), 0) == iota((ch, heads), 1), 1.0, 0.0).astype(BF), wh[...], ((1,), (1,)))
    zc = jnp.zeros((ch, ch), F32)

    def spread(tap):
        blocks = [[jnp.where(eye, tap(n, m), 0.0) for m in range(3)] + [zc] for n in range(3)]
        blocks.append([zc, zc, zc, whs])
        return jnp.concatenate([jnp.concatenate(b, axis=1) for b in blocks], axis=0)

    for sums, z, out, length, weights in (
        (rsv, zl, plx, tr, spread(lambda b, a: taps[a][b])),
        (cst, zr, prx, tc, spread(lambda a, b: taps[a][b])),
    ):
        z[:16, :] = jnp.zeros((16, 4 * ch), F32)
        z[16 + length :, :] = jnp.zeros((16, 4 * ch), F32)
        z[16 : 16 + length, :] = dotf(sums, weights, precision=HI)
        ext = z[8 : 24 + length, 3 * ch :]
        for n in range(3):
            ext = ext + z[12 - STEP * n : 28 - STEP * n + length, n * ch : (n + 1) * ch]
        out[...] = ext


def tile(scale, lext, rext, dk, wp, wh, cot):
    ch, heads = wh.shape
    tr, tc = cot.shape[1:]
    cg, hg, groups = ch * GR, heads * GR, tr // GR
    vm = pl.BlockSpec(memory_space=pltpu.VMEM)
    return pl.pallas_call(
        functools.partial(tile_kernel, scale),
        out_shape=(
            jax.ShapeDtypeStruct((tr + 16, ch), F32),
            jax.ShapeDtypeStruct((tc + 16, ch), F32),
            jax.ShapeDtypeStruct((ch + 8, 4 * ch), F32),
        ),
        in_specs=[vm] * 6,
        out_specs=(vm,) * 3,
        scratch_shapes=[
            pltpu.VMEM((tr, 8 * ch), BF),
            pltpu.VMEM((8 * ch, tc), BF),
            pltpu.VMEM((cg, hg), BF),
            pltpu.VMEM((cg, 8 * ch), BF),
            pltpu.VMEM((2, tc, 4 * ch), BF),
            pltpu.VMEM((3, 4 * ch, cg), BF),
            pltpu.VMEM((4 * ch, hg), BF),
            pltpu.VMEM((tr, 4 * ch), F32),
            pltpu.VMEM((4 * ch, tc), F32),
            pltpu.VMEM((cg, tc), BF),
            pltpu.VMEM((cg, groups * tc), BF),
            pltpu.VMEM((hg, groups * tc), BF),
            pltpu.VMEM((tr + 32, 4 * ch), F32),
            pltpu.VMEM((tc + 32, 4 * ch), F32),
        ],
        compiler_params=pltpu.CompilerParams(vmem_limit_bytes=48 * 1024 * 1024),
    )(lext, rext, dk, wp, wh, cot)


def body(bin_features, w_left, w_right, depth_kernel, w_point, w_head, cotangent):
    ch, heads = w_head.shape
    tr, tc = cotangent.shape[1:]
    nb = tr * lax.axis_size("row")
    scale = 1.0 / math.sqrt(nb)
    row, col = lax.axis_index("row"), lax.axis_index("col")
    feats = lax.all_gather(bin_features, "row", axis=0, tiled=True)
    both = dotf(feats, jnp.concatenate([w_left, w_right], axis=1)).astype(BF).astype(F32)
    both = jnp.pad(both, ((8, 8), (0, 0)))
    lext = lax.dynamic_slice(both, (row * tr, 0), (tr + 16, ch))
    rext = lax.dynamic_slice(both, (col * tc, ch), (tc + 16, ch))
    plx, prx, small = tile(scale, lext, rext, depth_kernel, w_point, w_head, cotangent)
    full_l = lax.dynamic_update_slice(jnp.zeros((nb + 16, ch), F32), plx, (row * tr, 0))
    full_r = lax.dynamic_update_slice(jnp.zeros((nb + 16, ch), F32), prx, (col * tc, 0))
    full = jnp.concatenate([full_l, full_r], axis=1)
    full, small = lax.psum((full, small), ("row", "col"))
    grads = full[8 : 8 + nb].astype(BF)
    grad_features = dotf(
        lax.dynamic_slice(grads, (row * tr, 0), (tr, 2 * ch)),
        jnp.concatenate([w_left, w_right], axis=1), ((1,), (1,))).astype(BF)
    gw = scale * dotf(feats, grads, ((0,), (0,)))
    hc, pc = small[:ch, :heads], small[:ch, ch : ch + heads]
    gk = small[ch : ch + 3, : 3 * ch].reshape(3, 3, ch) + small[ch + 3 : ch + 6, : 3 * ch].reshape(3, 3, ch).transpose(1, 0, 2)
    grad_point = scale * scale * dotf(hc, w_head.astype(F32), ((1,), (1,)), HI)
    grad_head = scale * (pc + dotf(w_point.astype(F32), hc, ((0,), (0,)), HI))
    return grad_features, gw[:, :ch], gw[:, ch:], scale * gk.reshape(9, ch), grad_point, grad_head


def solution(mesh):
    return jax.shard_map(
        body,
        mesh=mesh,
        in_specs=(P("row", None), P(), P(), P(), P(), P(), P(None, "row", "col")),
        out_specs=(P("row", None), P(), P(), P(), P(), P()),
        check_vma=False,
    )
```

time: 294 us -> 117 us (0.40)
  blocking collectives: 114 us -> 46.9 us
  other arithmetic: 39 us -> 0.25 us
  local copies, waits for them, and re-layouts: 34 us -> 4.96 us
  matrix products: 28.2 us -> 3.82 us
  waiting for transfers between devices: 47.7 us -> 29.5 us
  Pallas kernels: 0 us -> 17.2 us
  starting transfers between devices: 15.5 us -> 0.04 us
    psum x4 -> x1, blocking collectives: 102 us -> 46.9 us  [body(): full, small = lax.psum((full, small), ('row', 'col'))]
    psum x1 -> x0, waiting for transfers between devices: 38.8 us -> none  [body(): wleft_sum, wright_sum = lax.psum((wleft_part, wright_part), 'row')]
    all_gather x0 -> x1, waiting for transfers between devices: none -> 28.9 us  [body(): feats = lax.all_gather(bin_features, 'row', axis=0, tiled=True)]
    dot_general x10 -> x5, matrix products: 28.2 us -> 3.82 us  [dotf(): lax.dot_general(a, b, (contract, ((), ())), precision=precision, preferre...]
    slice x8 -> x3, local copies, waits for them, and re-layouts: 21.2 us -> 0.68 us  [the longest x1 0.66 us: body(): gw[:, ch:]]
    pallas_call x0 -> x1, Pallas kernels: none -> 17.2 us  [tile(): pl.pallas_call(functools.partial(tile_kernel, scale), out_shape=(jax.Shap...]
    concatenate x4 -> x1, other arithmetic: 16.6 us -> 0.21 us  [body(): full = jnp.concatenate([full_l, full_r], axis=1)]
    ppermute x8 -> x0, starting transfers between devices: 15.5 us -> none  [the longest x4 10.1 us: extended(): before = lax.ppermute(last, axis, up)]
  transfers between devices with their start and end apart: 9 -> 1, of which waited for: 5 -> 1; matrix products, arithmetic and copies ran while one was open for 4% -> 2% of each run, Pallas kernels for 0% -> 0%
where the time goes in v1:
time: 117 us
  blocking collectives  46.9 us (40%)
  waiting for transfers between devices  29.5 us (25%)
  Pallas kernels  17.2 us (15%)
  between operations  14.2 us (12%)
  local copies, waits for them, and re-layouts  4.96 us (4%)
  matrix products  3.82 us (3%)
    psum x1, blocking collectives, body(): full, small = lax.psum((full, small), ('row', 'col'))  46.9 us
    all_gather x1, waiting for transfers between devices, body(): feats = lax.all_gather(bin_features, 'row', axis=0, tiled=True)  28.9 us
    pallas_call x1, Pallas kernels, tile(): pl.pallas_call(functools.partial(tile_kernel, scale), out_shape=(jax.Shap...  17.2 us
    dot_general x5, matrix products, dotf(): lax.dot_general(a, b, (contract, ((), ())), precision=precision, preferre...  3.82 us
    unnamed x13, local copies, waits for them, and re-layouts  2.34 us
  transfers between devices with their start and end apart: 1, of which 1 were waited for; matrix products, arithmetic and copies ran while one was open for 2% of the time, Pallas kernels for 0%

profile of v1, /device:TPU:0, one launch (start us, length us, event | category | flops | bytes accessed | tf_op | source)
XLA Modules:
  0.0 116.9 jit_solution(10106511553720657746)
XLA Ops:
  7.2 0.0 all-gather.2.cloned.1.call-start
  7.2 0.7 all-gather.2.cloned.1.call-update
  7.9 0.0 copy-start
  7.9 0.0 copy-start.1
  7.9 0.0 copy-start.2
  7.9 0.9 copy.20.wh
  8.8 0.8 constant_dynamic-update-slice_fusion.1
  9.6 0.8 constant_dynamic-update-slice_fusion
  10.3 28.9 %all-gather.2.cloned.1.call-done = bf16[1024,512]{1,0:T(8,128)(2,1)} async-done(((bf16[256,512]{1,0:T(8,128)(2,1)}), bf16[1024,512]{1,0:T(8,128)(2,1)}) %all-gather.2.cloned.1.call-update) | async-done | bytes 1048592 | tf_op jit(solution)/shard_map/all_gather | solution.py:199
  39.2 1.7 %convolution_convert_fusion.1 = bf16[64,1024]{1,0:T(8,128)(2,1)S(1)} fusion(bf16[512,64]{0,1:T(8,128)(2,1)S(1)} %constant_dynamic-update-slice_fusion, bf16[1024,512]{1,0:T(8,128)(2,1)} %all-gather.2.cloned.1.call-done), kind=kOutput, calls=%fused_computation.1 | convolution fusion | flops 67174400 | bytes 1245184 | tf_op jit(solution)/shard_map/dot_general | solution.py:28
  40.9 0.2 copy.19
  41.1 0.1 constant_dynamic-slice_fusion.1.rext
  41.2 0.0 copy-done
  41.2 0.0 copy-done.1
  41.2 0.0 copy-done.2
  41.2 17.2 %shard_map.118 = (f32[272,32]{1,0:T(8,128)S(1)}, f32[144,32]{1,0:T(8,128)S(1)}, f32[40,128]{1,0:T(8,128)S(1)}) custom-call(f32[272,32]{1,0:T(8,128)S(1)} %constant_dynamic-slice_fusion.lext, f32[144,32]{1,0:T(8,128)S(1)} %constant_dynamic-slice_fusion.1.rext, f32[9,32]{1,0:T(8,128)S(1)} %copy-done.1, bf16[32,32]{1,0:T(8,128)(2,1)S(1)} %copy-done.2, ...), custom_call_target="tpu_custom_call" | custom-call | tf_op jit(solution)/shard_map/pallas_call | solution.py:164
  58.5 0.0 copy-start.4
  58.5 0.0 copy-start.3
  58.6 0.2 pad_maximum_fusion
  58.8 46.9 %all-reduce.3 = (bf16[1040,64]{1,0:T(8,128)(2,1)S(1)}, f32[40,128]{1,0:T(8,128)S(1)}) all-reduce(f32[1040,64]{1,0:T(8,128)S(1)} %pad_maximum_fusion, f32[40,128]{1,0:T(8,128)S(1)} %get-tuple-element.11), channel_id=1, replica_groups=mesh['row'=4,'col'=8] {'row','col'}, use_global_device_ids=true, to_apply=%region_0.1 | all-reduce | flops 71680 | bytes 440320 | tf_op jit(solution)/shard_map/psum | solution.py:208
  105.7 0.2 fusion.2
  105.9 0.0 copy-done.4
  105.9 0.7 convolution_multiply_fusion.1
  106.7 0.1 reshape.21
  106.8 0.1 reshape.22
  106.9 0.6 mul.46
  107.5 0.0 copy-done.3
  107.5 0.3 fusion
  107.8 0.7 fusion.8
  108.5 0.7 copy.24
  109.2 0.9 convolution_convert_fusion
  (10 shorter events, 0.2 us)
Async XLA Ops:
  7.2 32.0 %all-gather.2.cloned.1.call-start = ((), (), s32[]{:S(2)}) async-start(), calls=%async_computation | async-start | bytes 1310720 | tf_op jit(solution)/shard_map/all_gather | solution.py:199
  7.9 33.3 %copy-start = (bf16[24,256,128]{2,1,0:T(8,128)(2,1)S(1)}, bf16[24,256,128]{2,1,0:T(8,128)(2,1)}, u32[]{:S(2)}) copy-start(bf16[24,256,128]{2,1,0:T(8,128)(2,1)} %cot.1) | copy-start | bytes 4718596
  7.9 33.3 %copy-start.1 = (f32[9,32]{1,0:T(8,128)S(1)}, f32[9,32]{1,0:T(8,128)}, u32[]{:S(2)}) copy-start(f32[9,32]{1,0:T(8,128)} %dk.1) | copy-start | bytes 3460
  7.9 33.3 %copy-start.2 = (bf16[32,32]{1,0:T(8,128)(2,1)S(1)}, bf16[32,32]{1,0:T(8,128)(2,1)}, u32[]{:S(2)}) copy-start(bf16[32,32]{1,0:T(8,128)(2,1)} %wp.1) | copy-start | bytes 6148
  58.5 47.5 %copy-start.4 = (bf16[32,24]{0,1:T(8,128)(2,1)S(1)}, bf16[32,24]{0,1:T(8,128)(2,1)}, u32[]{:S(2)}) copy-start(bf16[32,24]{0,1:T(8,128)(2,1)} %param.12) | copy-start | bytes 4612
  58.5 49.0 %copy-start.3 = (bf16[1024,512]{1,0:T(8,128)(2,1)S(1)}, bf16[1024,512]{1,0:T(8,128)(2,1)}, u32[]{:S(2)}) copy-start(bf16[1024,512]{1,0:T(8,128)(2,1)} %all-gather.2.cloned.1.call-done) | copy-start | bytes 3145732
Sparse Core Ops, SparseCore 0:
  9.8 29.3 all-gather.1

commit v2 on v1

v2 whole, which is shorter than its diff:
```python
import functools
import math

import jax
import jax.numpy as jnp
from jax import lax
from jax.experimental import pallas as pl
from jax.experimental.pallas import tpu as pltpu
from jax.sharding import PartitionSpec as P

STEP = 4
BF = jnp.bfloat16
F32 = jnp.float32
HI = lax.Precision.HIGHEST
GR = 16


def iota(shape, dim):
    return lax.broadcasted_iota(jnp.int32, shape, dim)


def split(x):
    hi = x.astype(BF)
    return hi, (x - hi.astype(F32)).astype(BF)


def dotf(a, b, contract=((1,), (0,)), precision=None):
    return lax.dot_general(a, b, (contract, ((), ())), precision=precision, preferred_element_type=F32)


MESH = pl.DeviceIdType.MESH


def pack(x):
    n = x.shape[0] // 4
    return jnp.concatenate([x[k * n : (k + 1) * n] for k in range(4)], axis=1)


def unpack(x):
    n = x.shape[1] // 4
    return jnp.concatenate([x[:, k * n : (k + 1) * n] for k in range(4)], axis=0)


def tile_kernel(scale, feats, wl, wr, dk, wp, wh, cot, gf_out, gwl_out, gwr_out, gk_out, gp_out, gh_out,
                lext, rext, plx, prx, small, qs, ns, k2, cm, es, ecol, ecx, rs, cs, gcs, hid, xs, zl, zr,
                proj, lbuf, rbuf, colsend, colrecv, rowsend, rowrecv, halosend, halorecv,
                agsend, agrecv, spsend, sprecv, sfin, gwsend, gwrecv, window,
                rseg_send, rseg_recv, lseg_send, lseg_recv, c1s, c1r, r1s, r1r, h1s, h1r,
                c2s, c2r, r2s, r2r, c3s, c3r, r3s, r3r, local_sem):
    ch, heads = wh.shape
    tr, tc = cot.shape[1:]
    groups = tr // GR
    cg, hg = ch * GR, heads * GR
    row, col = lax.axis_index("row"), lax.axis_index("col")
    row_first, row_last = row == 0, row == lax.axis_size("row") - 1
    col_first, col_last = col == 0, col == lax.axis_size("col") - 1
    taps = [[dk[3 * a + b : 3 * a + b + 1, :] for b in range(3)] for a in range(3)]

    def edge(first, last, pos, length):
        return ((pos < STEP) & first) | ((pos >= length - STEP) & last)

    n_row, n_col = lax.axis_size("row"), lax.axis_size("col")
    nb = tr * n_row
    row_mates = [lax.rem(row + k, n_row) for k in range(1, n_row)]
    col_mates = [lax.rem(col + k, n_col) for k in range(1, n_col)]

    lbuf[...] = jnp.zeros_like(lbuf)
    halorecv[...] = jnp.zeros_like(halorecv)
    for first, count in ((0, 16), (16 + tc, 16)):
        rbuf[first : first + count, :] = jnp.zeros((count, 4 * ch), BF)
    barrier = pltpu.get_barrier_semaphore()
    for m in row_mates:
        pl.semaphore_signal(barrier, inc=1, device_id=(m, col), device_id_type=MESH)
    for m in col_mates:
        pl.semaphore_signal(barrier, inc=1, device_id=(row, m), device_id_type=MESH)

    weights = jnp.concatenate([wl[...], wr[...], jnp.zeros((wl.shape[0], 2 * ch), BF)], axis=1)
    proj[...] = dotf(feats[...], weights).astype(BF)
    pl.semaphore_wait(barrier, n_row + n_col - 2)

    def remote(src, dst, send, recv, device):
        return pltpu.make_async_remote_copy(
            src_ref=src, dst_ref=dst, send_sem=send, recv_sem=recv, device_id=device, device_id_type=MESH)

    up = remote(proj.at[pl.ds(0, 16)], lbuf.at[1], lseg_send.at[0], lseg_recv.at[1], (row - 1, col))
    down = remote(proj.at[pl.ds(tr - 16, 16)], lbuf.at[0], lseg_send.at[1], lseg_recv.at[0], (row + 1, col))
    pl.when(row > 0)(up.start)
    pl.when(row < n_row - 1)(down.start)
    segments = []
    for k, (offset, first, count) in enumerate(((-16, 0, 16), (0, 16, tc), (tc, 16 + tc, 16))):
        bin0 = col * tc + offset
        inside = (bin0 >= 0) & (bin0 < nb)
        owner = lax.div(bin0 + nb, tr) - n_row
        local = pl.multiple_of(lax.rem(bin0 + nb, tr), 16)
        src = proj.at[pl.ds(local, count)]
        dst = rbuf.at[pl.ds(first, count)]
        own = inside & (owner == row)
        copies = [remote(src, dst, rseg_send.at[k, i], rseg_recv.at[k], (m, col)) for i, m in enumerate(row_mates)]
        keep = pltpu.make_async_copy(src, dst, local_sem.at[k])
        segments.append((inside, own, copies, keep))

        @pl.when(own)
        def _(copies=copies, keep=keep):
            for c in copies:
                c.start()
            keep.start()

    cm[...] = jnp.where(iota((cg, 8 * ch), 0) // GR == iota((cg, 8 * ch), 1) % ch, 1.0, 0.0).astype(BF)

    w2 = (0.5 * scale * dotf(wp[...], wh[...])).astype(BF)
    e_r = jnp.where(iota((cg, ch), 0) // GR == iota((cg, ch), 1), 1.0, 0.0).astype(BF)
    e_c = jnp.where(iota((heads, hg), 1) // GR == iota((heads, hg), 0), 1.0, 0.0).astype(BF)
    w2r = dotf(e_r, w2).astype(BF)
    same = iota((cg, hg), 0) % GR == iota((cg, hg), 1) % GR
    k2[...] = jnp.where(same, dotf(w2r, e_c), 0.0).astype(BF)

    jj, part = iota((tc, 4 * ch), 0), iota((tc, 4 * ch), 1) // ch
    drop = ((part == 0) & (jj < STEP) & col_first) | ((part == 2) & (jj >= tc - STEP) & col_last)
    es[0] = jnp.where(drop | (part == 3), 0.0, 1.0).astype(BF)
    es[1] = jnp.where(part == 3, 1.0, 0.0).astype(BF)
    pr, ci = iota((4 * ch, cg), 0), iota((4 * ch, cg), 1)
    mine = (pr % ch == ci // GR) & (pr // ch < 3)
    top = (pr // ch == 0) & (ci % GR < STEP) & row_first
    low = (pr // ch == 2) & (ci % GR >= GR - STEP) & row_last
    ecol[0] = jnp.where(mine & ~top, 1.0, 0.0).astype(BF)
    ecol[1] = jnp.where(mine, 1.0, 0.0).astype(BF)
    ecol[2] = jnp.where(mine & ~low, 1.0, 0.0).astype(BF)
    ecx[...] = jnp.where(
        iota((4 * ch, hg), 0) == 3 * ch + iota((4 * ch, hg), 1) // GR, 1.0, 0.0).astype(BF)
    for inside, own, copies, keep in segments:

        @pl.when(own)
        def _(copies=copies, keep=keep):
            keep.wait()
            for c in copies:
                c.wait_send()

        @pl.when(inside & jnp.logical_not(own))
        def _(copies=copies):
            copies[0].wait_recv()

    @pl.when(row > 0)
    def _():
        up.wait_send()
        down.wait_recv()

    @pl.when(row < n_row - 1)
    def _():
        down.wait_send()
        up.wait_recv()

    lext[0:16, :] = lbuf[0, :, :ch].astype(F32)
    lext[16 : 16 + tr, :] = proj[:, :ch].astype(F32)
    lext[16 + tr :, :] = lbuf[1, :, :ch].astype(F32)
    rext[...] = rbuf[:, ch : 2 * ch].astype(F32)

    l_sh = [lext[16 + STEP * (a - 1) : 16 + STEP * (a - 1) + tr, :] for a in range(3)]
    r_sh = [rext[16 + STEP * (b - 1) : 16 + STEP * (b - 1) + tc, :] for b in range(3)]
    a1 = sum(l_sh[a] * (taps[a][0] + taps[a][1] + taps[a][2]) for a in range(3))
    da0 = sum(l_sh[a] * taps[a][0] for a in range(3))
    da2 = sum(l_sh[a] * taps[a][2] for a in range(3))
    da = -jnp.where(col_first, da0, jnp.where(col_last, da2, jnp.zeros_like(da2)))
    b1 = sum(r_sh[b] * (taps[0][b] + taps[1][b] + taps[2][b]) for b in range(3))
    db0 = sum(r_sh[b] * taps[0][b] for b in range(3))
    db2 = sum(r_sh[b] * taps[2][b] for b in range(3))
    db = -jnp.where(row_first, db0, jnp.where(row_last, db2, jnp.zeros_like(db2)))
    rind = jnp.where(edge(row_first, row_last, iota((tr, 2 * ch), 0), tr), 1.0, 0.0).astype(BF)
    qs[...] = jnp.concatenate(
        [*split(0.5 * a1), *split(0.5 * da), jnp.ones((tr, 2 * ch), BF), rind], axis=1)
    b_parts = [p.astype(F32) for p in (*split(0.5 * b1), *split(0.5 * db))]
    ns[4 * ch :, :] = jnp.concatenate(b_parts, axis=1).T.astype(BF)
    ns[: 2 * ch, :] = jnp.ones((2 * ch, tc), BF)
    ns[2 * ch : 4 * ch, :] = jnp.where(
        edge(col_first, col_last, iota((2 * ch, tc), 1), tc), 1.0, 0.0).astype(BF)
    cs[...] = jnp.zeros_like(cs)

    chunk = 128
    lane_c = iota((1, 1, 4 * ch), 2) % ch

    def group(g, carry):
        start = pl.multiple_of(g * GR, GR)
        lanes = pl.ds(pl.multiple_of(g * tc, 128), tc)
        x = cot[:, pl.ds(start, GR), :].reshape(hg, tc)
        xs[:, lanes] = x
        q = qs[pl.ds(start, GR), :]
        total = jnp.zeros((GR, 4 * ch), F32)
        for k in range(cg // chunk):
            rows = slice(k * chunk, (k + 1) * chunk)
            n = chunk // GR
            m = (cm[rows, :].reshape(n, GR, 8 * ch) * q[None]).reshape(chunk, 8 * ch)
            u = dotf(m, ns[...])
            gh = dotf(k2[rows, :], x)
            t = jnp.tanh(u)
            p = 1.0 + t
            h = u * p
            gc = (gh * (p + h - h * t)).astype(BF)
            hid[rows, lanes] = h.astype(BF)
            gcs[rows, :] = gc
            y = dotf(gc, es[0]).reshape(n, GR, 4 * ch)
            pick = iota((n, 1, 4 * ch), 0) + k * n == lane_c
            total = total + jnp.sum(jnp.where(pick, y, 0.0), axis=0)
        y = dotf(x, es[1]).reshape(heads, GR, 4 * ch)
        total = total + jnp.sum(jnp.where(iota((heads, 1, 4 * ch), 0) == lane_c, y, 0.0), axis=0)
        rs[pl.ds(start, GR), :] = total
        kind = (g + groups - 1) // groups + g // (groups - 1)
        cs[...] += dotf(ecol[kind], gcs[...]) + dotf(ecx[...], x)
        return carry

    lax.fori_loop(0, groups, group, 0)

    prod = dotf(hid[...], xs[...], ((1,), (1,)))
    prod = jnp.sum(jnp.where(same, prod, 0.0).reshape(ch, GR, hg), axis=1)
    e_h = jnp.where(iota((hg, ch), 0) // GR == iota((hg, ch), 1), 1.0, 0.0)
    hc = dotf(prod, e_h, precision=HI)
    cst = cs[...].T
    rsv = rs[...]
    pc = dotf(l_sh[1], rsv[:, 3 * ch :], ((0,), (0,)), HI) + dotf(r_sh[1], cst[:, 3 * ch :], ((0,), (0,)), HI)
    small[:ch, :] = jnp.concatenate([hc, pc, jnp.zeros((ch, 2 * ch), F32)], axis=1)
    rows_out = []
    zero_l, zero_r = jnp.zeros((tr, ch), F32), jnp.zeros((tc, ch), F32)
    for a in range(3):
        rows_out.append(jnp.sum(jnp.concatenate([l_sh[a]] * 3 + [zero_l], axis=1) * rsv, axis=0, keepdims=True))
    for b in range(3):
        rows_out.append(jnp.sum(jnp.concatenate([r_sh[b]] * 3 + [zero_r], axis=1) * cst, axis=0, keepdims=True))
    small[ch : ch + 8, :] = jnp.concatenate(rows_out + [jnp.zeros((2, 4 * ch), F32)], axis=0)
    small[ch + 8 :, :] = jnp.zeros((ch - 8, 4 * ch), F32)

    eye = iota((ch, ch), 0) == iota((ch, ch), 1)
    whs = scale * dotf(jnp.where(iota((ch, heads), 0) == iota((ch, heads), 1), 1.0, 0.0).astype(BF), wh[...], ((1,), (1,)))
    zc = jnp.zeros((ch, ch), F32)

    def spread(tap):
        blocks = [[jnp.where(eye, tap(n, m), 0.0) for m in range(3)] + [zc] for n in range(3)]
        blocks.append([zc, zc, zc, whs])
        return jnp.concatenate([jnp.concatenate(b, axis=1) for b in blocks], axis=0)

    for sums, z, out, length, weights in (
        (rsv, zl, plx, tr, spread(lambda b, a: taps[a][b])),
        (cst, zr, prx, tc, spread(lambda a, b: taps[a][b])),
    ):
        z[:16, :] = jnp.zeros((16, 4 * ch), F32)
        z[16 + length :, :] = jnp.zeros((16, 4 * ch), F32)
        z[16 : 16 + length, :] = dotf(sums, weights, precision=HI)
        ext = z[8 : 24 + length, 3 * ch :]
        for n in range(3):
            ext = ext + z[12 - STEP * n : 28 - STEP * n + length, n * ch : (n + 1) * ch]
        out[...] = ext

    lanes = 4 * ch
    pp, sp = tr // 4 // n_col, 2 * ch // n_col
    colsend[:, :pp, :] = pack(plx[8 : 8 + tr, :]).reshape(n_col, pp, lanes)
    colsend[:, pp:, :] = small[...].reshape(n_col, sp, lanes)
    pad = jnp.zeros((8, 3 * ch), F32)
    halosend[0] = jnp.concatenate([plx[:8, :], pad], axis=1)
    halosend[1] = jnp.concatenate([plx[8 + tr :, :], pad], axis=1)
    pr = (tc + 16) // 4
    rowsend[...] = pack(prx[...])

    def to_col(src, dst, send, recv):
        return [remote(src(m), dst.at[col], send.at[m], recv.at[col], (row, m)) for m in col_mates]

    def to_row(src, dst, send, recv):
        return [remote(src, dst.at[row], send.at[m], recv.at[row], (m, col)) for m in row_mates]

    def from_col(src, dst, send, recv):
        return [remote(src(m), dst.at[m], send.at[m], recv.at[m], (row, m)) for m in col_mates]

    def from_row(src, dst, send, recv):
        return [remote(src, dst.at[m], send.at[m], recv.at[m], (m, col)) for m in row_mates]

    def start(copies):
        for c in copies:
            c.start()

    def arrived(copies):
        for c in copies:
            c.wait_recv()

    def sent(copies):
        for c in copies:
            c.wait_send()

    hup = remote(halosend.at[0], halorecv.at[1], h1s.at[0], h1r.at[1], (row - 1, col))
    hdown = remote(halosend.at[1], halorecv.at[0], h1s.at[1], h1r.at[0], (row + 1, col))
    p1c = (lambda m: colsend.at[m], colrecv, c1s, c1r)
    p1r = (rowsend, rowrecv, r1s, r1r)
    s1c, s1r = to_col(*p1c), to_row(*p1r)
    start(s1c)
    start(s1r)
    pl.when(row > 0)(hup.start)
    pl.when(row < n_row - 1)(hdown.start)
    arrived(from_col(*p1c))
    piece = colsend[col]
    for m in col_mates:
        piece = piece + colrecv[m]
    spsend[...] = piece[pp:]
    p2r = (spsend, sprecv, r2s, r2r)
    s2r = to_row(*p2r)
    start(s2r)
    arrived(from_row(*p1r))
    right = rowsend[...]
    for m in row_mates:
        right = right + rowrecv[m]

    @pl.when(row > 0)
    def _():
        hup.wait_send()
        hdown.wait_recv()

    @pl.when(row < n_row - 1)
    def _():
        hdown.wait_send()
        hup.wait_recv()

    fill = [jnp.zeros((agsend.shape[0] - pp - 4 - pr, lanes), F32)] if agsend.shape[0] > pp + 4 + pr else []
    agsend[...] = jnp.concatenate(
        [right, pack(halorecv[0, :, :ch]), pack(halorecv[1, :, :ch]), piece[:pp]] + fill, axis=0).astype(BF)
    p2c = (lambda m: agsend, agrecv, c2s, c2r)
    s2c = to_col(*p2c)
    start(s2c)
    sent(s1c)
    sent(s1r)
    arrived(from_row(*p2r))
    total = spsend[...]
    for m in row_mates:
        total = total + sprecv[m]
    sfin[col] = total
    p3c = (lambda m: sfin.at[col], sfin, c3s, c3r)
    s3c = to_col(*p3c)
    start(s3c)
    arrived(from_col(*p2c))
    sent(s2c)
    agrecv[col] = agsend[...]
    gl = unpack(jnp.concatenate([agrecv[m, pr + 4 : pr + 4 + pp, :].astype(F32) for m in range(n_col)], axis=0))
    halo = sum(agrecv[m, pr : pr + 4, :].astype(F32) for m in range(n_col))
    gl = jnp.concatenate([gl[:8] + unpack(halo[:2]), gl[8:-8], gl[-8:] + unpack(halo[2:])], axis=0)
    window[...] = jnp.zeros_like(window)
    for k in range(tr // tc + 2):
        m = lax.div(row * tr, tc) - 1 + k

        @pl.when((m >= 0) & (m < n_col))
        def _(m=m, k=k):
            window[k * tc : k * tc + tc + 16, :] += unpack(agrecv[m, :pr, :].astype(F32))

    gr = window[tc + 8 : tc + 8 + tr, :]
    glb, grb = gl.astype(BF), gr.astype(BF)
    both = jnp.concatenate([gl, gr, jnp.zeros((tr, 2 * ch), F32)], axis=1).T[: 2 * ch].astype(BF)
    part = scale * dotf(both, feats[...])

    gwsend[...] = part.astype(BF)
    p3r = (gwsend, gwrecv, r3s, r3r)
    s3r = to_row(*p3r)
    start(s3r)
    gf_out[...] = (dotf(glb, wl[...], ((1,), (1,))) + dotf(grb, wr[...], ((1,), (1,)))).astype(BF)
    arrived(from_col(*p3c))
    sent(s3c)
    sent(s2r)
    full = jnp.concatenate([sfin[m] for m in range(n_col)], axis=0)
    hc, pc = full[:ch, :heads], full[:ch, ch : ch + heads]
    for a in range(3):
        for b in range(3):
            gk_out[3 * a + b : 3 * a + b + 1, :] = scale * (
                full[ch + a : ch + a + 1, b * ch : (b + 1) * ch]
                + full[ch + 3 + b : ch + 4 + b, a * ch : (a + 1) * ch])
    gp_out[...] = scale * scale * dotf(hc, wh[...].astype(F32), ((1,), (1,)), HI)
    gh_out[...] = scale * (pc + dotf(wp[...].astype(F32), hc, ((0,), (0,)), HI))
    arrived(from_row(*p3r))
    for m in row_mates:
        part = part + gwrecv[m].astype(F32)
    part = part.T
    gwl_out[...] = part[:, :ch]
    gwr_out[...] = part[:, ch:]
    sent(s3r)


def body(bin_features, w_left, w_right, depth_kernel, w_point, w_head, cotangent):
    ch, heads = w_head.shape
    tr, tc = cotangent.shape[1:]
    n_row, n_col = lax.axis_size("row"), lax.axis_size("col")
    scale = 1.0 / math.sqrt(tr * n_row)
    cg, hg, groups = ch * GR, heads * GR, tr // GR
    d, lanes = w_left.shape[0], 4 * ch
    pp, sp, pr = tr // 4 // n_col, 2 * ch // n_col, (tc + 16) // 4
    ag = -(-(pp + 4 + pr) // 16) * 16
    vm = pl.BlockSpec(memory_space=pltpu.VMEM)
    dma = pltpu.SemaphoreType.DMA
    return pl.pallas_call(
        functools.partial(tile_kernel, scale),
        out_shape=(
            jax.ShapeDtypeStruct((tr, d), BF),
            jax.ShapeDtypeStruct((d, ch), F32),
            jax.ShapeDtypeStruct((d, ch), F32),
            jax.ShapeDtypeStruct((9, ch), F32),
            jax.ShapeDtypeStruct((ch, ch), F32),
            jax.ShapeDtypeStruct((ch, heads), F32),
        ),
        in_specs=[vm] * 7,
        out_specs=(vm,) * 6,
        scratch_shapes=[
            pltpu.VMEM((tr + 32, ch), F32),
            pltpu.VMEM((tc + 32, ch), F32),
            pltpu.VMEM((tr + 16, ch), F32),
            pltpu.VMEM((tc + 16, ch), F32),
            pltpu.VMEM((2 * ch, lanes), F32),
            pltpu.VMEM((tr, 8 * ch), BF),
            pltpu.VMEM((8 * ch, tc), BF),
            pltpu.VMEM((cg, hg), BF),
            pltpu.VMEM((cg, 8 * ch), BF),
            pltpu.VMEM((2, tc, 4 * ch), BF),
            pltpu.VMEM((3, 4 * ch, cg), BF),
            pltpu.VMEM((4 * ch, hg), BF),
            pltpu.VMEM((tr, 4 * ch), F32),
            pltpu.VMEM((4 * ch, tc), F32),
            pltpu.VMEM((cg, tc), BF),
            pltpu.VMEM((cg, groups * tc), BF),
            pltpu.VMEM((hg, groups * tc), BF),
            pltpu.VMEM((tr + 32, 4 * ch), F32),
            pltpu.VMEM((tc + 32, 4 * ch), F32),
            pltpu.VMEM((tr, lanes), BF),
            pltpu.VMEM((2, 16, lanes), BF),
            pltpu.VMEM((tc + 32, lanes), BF),
            pltpu.VMEM((n_col, pp + sp, lanes), F32),
            pltpu.VMEM((n_col, pp + sp, lanes), F32),
            pltpu.VMEM((pr, lanes), F32),
            pltpu.VMEM((n_row, pr, lanes), F32),
            pltpu.VMEM((2, 8, lanes), F32),
            pltpu.VMEM((2, 8, lanes), F32),
            pltpu.VMEM((ag, lanes), BF),
            pltpu.VMEM((n_col, ag, lanes), BF),
            pltpu.VMEM((sp, lanes), F32),
            pltpu.VMEM((n_row, sp, lanes), F32),
            pltpu.VMEM((n_col, sp, lanes), F32),
            pltpu.VMEM((2 * ch, d), BF),
            pltpu.VMEM((n_row, 2 * ch, d), BF),
            pltpu.VMEM((tr + 2 * tc + 16, ch), F32),
            dma((3, n_row)), dma((3,)), dma((2,)), dma((2,)),
            dma((n_col,)), dma((n_col,)), dma((n_row,)), dma((n_row,)), dma((2,)), dma((2,)),
            dma((n_col,)), dma((n_col,)), dma((n_row,)), dma((n_row,)),
            dma((n_col,)), dma((n_col,)), dma((n_row,)), dma((n_row,)),
            dma((3,)),
        ],
        compiler_params=pltpu.CompilerParams(
            vmem_limit_bytes=48 * 1024 * 1024, collective_id=0, has_side_effects=True),
    )(bin_features, w_left, w_right, depth_kernel, w_point, w_head, cotangent)


def solution(mesh):
    return jax.shard_map(
        body,
        mesh=mesh,
        in_specs=(P("row", None), P(), P(), P(), P(), P(), P(None, "row", "col")),
        out_specs=(P("row", None), P(), P(), P(), P(), P()),
        check_vma=False,
    )
```

time: 117 us -> 51.9 us (0.44)
  blocking collectives: 46.9 us -> 0 us
  waiting for transfers between devices: 29.5 us -> 0 us
  Pallas kernels: 17.2 us -> 40.5 us
  between operations: 14.2 us -> 0.66 us
  local copies, waits for them, and re-layouts: 4.96 us -> 10.3 us
  matrix products: 3.82 us -> 0 us
    psum x1 -> x0, blocking collectives: 46.9 us -> none  [body(): full, small = lax.psum((full, small), ('row', 'col'))]
    all_gather x1 -> x0, waiting for transfers between devices: 28.9 us -> none  [body(): feats = lax.all_gather(bin_features, 'row', axis=0, tiled=True)]
    pallas_call x1, Pallas kernels: 17.2 us -> 40.5 us  [body(): pl.pallas_call(functools.partial(tile_kernel, scale), out_shape=(jax.Shap...]
    unnamed x13 -> x14, local copies, waits for them, and re-layouts: 2.34 us -> 8.19 us
    dot_general x5 -> x0, matrix products: 3.82 us -> none  [dotf(): lax.dot_general(a, b, (contract, ((), ())), precision=precision, preferre...]
    pallas_call x0 -> x3, local copies, waits for them, and re-layouts: none -> 2.15 us  [body(): pl.pallas_call(functools.partial(tile_kernel, scale), out_shape=(jax.Shap...]
  transfers between devices with their start and end apart: 1 -> 0, of which waited for: 1 -> 0; matrix products, arithmetic and copies ran while one was open for 2% -> 0% of each run, Pallas kernels for 0% -> 0%
where the time goes in v2:
time: 51.9 us; the launch traced here: 51.5 us
  Pallas kernels  40.5 us (78%)
  local copies, waits for them, and re-layouts  10.3 us (20%)
  between operations  0.66 us (1%)
    pallas_call x1, Pallas kernels, body(): pl.pallas_call(functools.partial(tile_kernel, scale), out_shape=(jax.Shap...  40.5 us
    unnamed x14, local copies, waits for them, and re-layouts  8.19 us
    pallas_call x3, local copies, waits for them, and re-layouts, body(): pl.pallas_call(functools.partial(tile_kernel, scale), out_shape=(jax.Shap...  2.15 us

profile of v2, /device:TPU:0, one launch (start us, length us, event | category | flops | bytes accessed | tf_op | source)
XLA Modules:
  0.0 51.5 jit_solution(5686468267273586299)
XLA Ops:
  0.6 0.8 %copy.15.wh = bf16[32,24]{1,0:T(8,128)(2,1)S(1)} copy(bf16[32,24]{0,1:T(8,128)(2,1)} %param.12) | data formatting | bytes 3072 | tf_op args[5]
  1.4 0.9 %copy.13.wl = bf16[512,32]{1,0:T(8,128)(2,1)S(1)} copy(bf16[512,32]{0,1:T(8,128)(2,1)} %param.8) | data formatting | bytes 65536 | tf_op args[1]
  2.3 0.9 %copy.14.wr = bf16[512,32]{1,0:T(8,128)(2,1)S(1)} copy(bf16[512,32]{0,1:T(8,128)(2,1)} %param.9) | data formatting | bytes 65536 | tf_op args[2]
  3.2 0.0 copy-start
  3.2 1.4 %copy-done = bf16[24,256,128]{2,1,0:T(8,128)(2,1)S(1)} copy-done((bf16[24,256,128]{2,1,0:T(8,128)(2,1)S(1)}, bf16[24,256,128]{2,1,0:T(8,128)(2,1)}, u32[]{:S(2)}) %copy-start) | copy-done | bytes 1572888
  4.6 0.0 copy-start.1
  4.6 0.9 %copy-done.1 = bf16[256,512]{1,0:T(8,128)(2,1)S(1)} copy-done((bf16[256,512]{1,0:T(8,128)(2,1)S(1)}, bf16[256,512]{1,0:T(8,128)(2,1)}, u32[]{:S(2)}) %copy-start.1) | copy-done | bytes 262168
  5.5 0.0 copy-start.2
  5.5 0.7 %copy-done.2 = f32[9,32]{1,0:T(8,128)S(1)} copy-done((f32[9,32]{1,0:T(8,128)S(1)}, f32[9,32]{1,0:T(8,128)}, u32[]{:S(2)}) %copy-start.2) | copy-done | bytes 1176
  6.2 0.0 copy-start.3
  6.2 0.7 %copy-done.3 = bf16[32,32]{1,0:T(8,128)(2,1)S(1)} copy-done((bf16[32,32]{1,0:T(8,128)(2,1)S(1)}, bf16[32,32]{1,0:T(8,128)(2,1)}, u32[]{:S(2)}) %copy-start.3) | copy-done | bytes 2072
  6.9 40.5 %shard_map.118 = (bf16[256,512]{1,0:T(8,128)(2,1)S(1)}, f32[512,32]{1,0:T(8,128)S(1)}, f32[512,32]{1,0:T(8,128)S(1)}, f32[9,32]{1,0:T(8,128)S(1)}, f32[32,32]{1,0:T(8,128)S(1)}, /*index=5*/f32[32,24]{1,0:T(8,128)S(1)}) custom-call(bf16[256,512]{1,0:T(8,128)(2,1)S(1)} %copy-done.1, bf16[512,32]{1,0:T(8,128)(2,1)S(1)} %copy.13.wl, ...), custom_call_target="tpu_custom_call" | custom-call | tf_op jit(solution)/shard_map/pallas_call | solution.py:387
  47.4 0.7 %copy.18 = f32[32,24]{0,1:T(8,128)} copy(f32[32,24]{1,0:T(8,128)S(1)} %get-tuple-element.11) | data formatting | bytes 6144 | tf_op jit(solution)/shard_map/pallas_call | solution.py:387
  48.1 0.7 %copy.16 = f32[512,32]{0,1:T(8,128)} copy(f32[512,32]{1,0:T(8,128)S(1)} %get-tuple-element.7) | data formatting | bytes 131072 | tf_op jit(solution)/shard_map/pallas_call | solution.py:387
  48.8 0.7 %copy.17 = f32[512,32]{0,1:T(8,128)} copy(f32[512,32]{1,0:T(8,128)S(1)} %get-tuple-element.8) | data formatting | bytes 131072 | tf_op jit(solution)/shard_map/pallas_call | solution.py:387
  49.6 0.7 %copy.22 = bf16[256,512]{1,0:T(8,128)(2,1)} copy(bf16[256,512]{1,0:T(8,128)(2,1)S(1)} %get-tuple-element.18) | data formatting | bytes 524288
  50.3 0.6 %copy.23 = f32[9,32]{1,0:T(8,128)} copy(f32[9,32]{1,0:T(8,128)S(1)} %get-tuple-element.21) | data formatting | bytes 2304
  50.9 0.6 %copy.24 = f32[32,32]{1,0:T(8,128)} copy(f32[32,32]{1,0:T(8,128)S(1)} %get-tuple-element.22) | data formatting | bytes 8192
Async XLA Ops:
  3.2 1.4 %copy-start = (bf16[24,256,128]{2,1,0:T(8,128)(2,1)S(1)}, bf16[24,256,128]{2,1,0:T(8,128)(2,1)}, u32[]{:S(2)}) copy-start(bf16[24,256,128]{2,1,0:T(8,128)(2,1)} %cot.1) | copy-start | bytes 4718596
  4.6 0.9 %copy-start.1 = (bf16[256,512]{1,0:T(8,128)(2,1)S(1)}, bf16[256,512]{1,0:T(8,128)(2,1)}, u32[]{:S(2)}) copy-start(bf16[256,512]{1,0:T(8,128)(2,1)} %feats.1) | copy-start | bytes 786436
  5.5 0.7 %copy-start.2 = (f32[9,32]{1,0:T(8,128)S(1)}, f32[9,32]{1,0:T(8,128)}, u32[]{:S(2)}) copy-start(f32[9,32]{1,0:T(8,128)} %dk.1) | copy-start | bytes 3460
  6.2 0.7 %copy-start.3 = (bf16[32,32]{1,0:T(8,128)(2,1)S(1)}, bf16[32,32]{1,0:T(8,128)(2,1)}, u32[]{:S(2)}) copy-start(bf16[32,32]{1,0:T(8,128)(2,1)} %wp.1) | copy-start | bytes 6148

commit v3 on v2

--- a/solution.py
+++ b/solution.py
@@ -41,21 +41,25 @@
     return jnp.concatenate([x[:, k * n : (k + 1) * n] for k in range(4)], axis=0)
 
 
-def tile_kernel(scale, feats, wl, wr, dk, wp, wh, cot, gf_out, gwl_out, gwr_out, gk_out, gp_out, gh_out,
+def tile_kernel(scale, feats_hbm, wl_hbm, wr_hbm, dk_hbm, wp_hbm, wh_hbm, cot_hbm,
+                gf_out, gwl_out, gwr_out, gk_out, gp_out, gh_out,
+                feats, wl, wr, dk, wp, wh, cot, load_sem, ghs,
                 lext, rext, plx, prx, small, qs, ns, k2, cm, es, ecol, ecx, rs, cs, gcs, hid, xs, zl, zr,
                 proj, lbuf, rbuf, colsend, colrecv, rowsend, rowrecv, halosend, halorecv,
                 agsend, agrecv, spsend, sprecv, sfin, gwsend, gwrecv, window,
                 rseg_send, rseg_recv, lseg_send, lseg_recv, c1s, c1r, r1s, r1r, h1s, h1r,
                 c2s, c2r, r2s, r2r, c3s, c3r, r3s, r3r, local_sem):
-    ch, heads = wh.shape
+    loads = [pltpu.make_async_copy(src, dst, load_sem.at[k]) for k, (src, dst) in enumerate((
+        (feats_hbm, feats), (wl_hbm, wl), (wr_hbm, wr), (dk_hbm, dk), (wp_hbm, wp), (wh_hbm, wh), (cot_hbm, cot)))]
+    for copy in loads:
+        copy.start()
+    heads, ch = wh.shape
     tr, tc = cot.shape[1:]
     groups = tr // GR
     cg, hg = ch * GR, heads * GR
     row, col = lax.axis_index("row"), lax.axis_index("col")
     row_first, row_last = row == 0, row == lax.axis_size("row") - 1
     col_first, col_last = col == 0, col == lax.axis_size("col") - 1
-    taps = [[dk[3 * a + b : 3 * a + b + 1, :] for b in range(3)] for a in range(3)]
-
     def edge(first, last, pos, length):
         return ((pos < STEP) & first) | ((pos >= length - STEP) & last)
 
@@ -74,8 +78,12 @@
     for m in col_mates:
         pl.semaphore_signal(barrier, inc=1, device_id=(row, m), device_id_type=MESH)
 
-    weights = jnp.concatenate([wl[...], wr[...], jnp.zeros((wl.shape[0], 2 * ch), BF)], axis=1)
-    proj[...] = dotf(feats[...], weights).astype(BF)
+    for copy in loads[:6]:
+        copy.wait()
+    taps = [[dk[3 * a + b : 3 * a + b + 1, :] for b in range(3)] for a in range(3)]
+
+    weights = jnp.concatenate([wl[...], wr[...], jnp.zeros((2 * ch, wl.shape[1]), BF)], axis=0)
+    proj[...] = dotf(feats[...], weights, ((1,), (1,))).astype(BF)
     pl.semaphore_wait(barrier, n_row + n_col - 2)
 
     def remote(src, dst, send, recv, device):
@@ -107,17 +115,19 @@
 
     cm[...] = jnp.where(iota((cg, 8 * ch), 0) // GR == iota((cg, 8 * ch), 1) % ch, 1.0, 0.0).astype(BF)
 
-    w2 = (0.5 * scale * dotf(wp[...], wh[...])).astype(BF)
+    w2 = (0.5 * scale * dotf(wp[...], wh[...], ((1,), (1,)))).astype(BF)
     e_r = jnp.where(iota((cg, ch), 0) // GR == iota((cg, ch), 1), 1.0, 0.0).astype(BF)
     e_c = jnp.where(iota((heads, hg), 1) // GR == iota((heads, hg), 0), 1.0, 0.0).astype(BF)
     w2r = dotf(e_r, w2).astype(BF)
     same = iota((cg, hg), 0) % GR == iota((cg, hg), 1) % GR
     k2[...] = jnp.where(same, dotf(w2r, e_c), 0.0).astype(BF)
 
-    jj, part = iota((tc, 4 * ch), 0), iota((tc, 4 * ch), 1) // ch
+    jj, part = iota((2 * tc, 8 * ch), 0), iota((2 * tc, 8 * ch), 1)
+    paired = jj // tc == part // (4 * ch)
+    jj, part = jj % tc, part % (4 * ch) // ch
     drop = ((part == 0) & (jj < STEP) & col_first) | ((part == 2) & (jj >= tc - STEP) & col_last)
-    es[0] = jnp.where(drop | (part == 3), 0.0, 1.0).astype(BF)
-    es[1] = jnp.where(part == 3, 1.0, 0.0).astype(BF)
+    es[0] = jnp.where(paired & ~drop & (part != 3), 1.0, 0.0).astype(BF)
+    es[1] = jnp.where(paired & (part == 3), 1.0, 0.0).astype(BF)
     pr, ci = iota((4 * ch, cg), 0), iota((4 * ch, cg), 1)
     mine = (pr % ch == ci // GR) & (pr // ch < 3)
     top = (pr // ch == 0) & (ci % GR < STEP) & row_first
@@ -127,6 +137,27 @@
     ecol[2] = jnp.where(mine & ~low, 1.0, 0.0).astype(BF)
     ecx[...] = jnp.where(
         iota((4 * ch, hg), 0) == 3 * ch + iota((4 * ch, hg), 1) // GR, 1.0, 0.0).astype(BF)
+    cs[...] = jnp.zeros_like(cs)
+    lane_c = iota((1, 1, 8 * ch), 2) % ch
+    loads[6].wait()
+
+    def ahead(g, carry):
+        start = pl.multiple_of(g * 2 * GR, 2 * GR)
+        lanes = pl.ds(pl.multiple_of(g * 2 * tc, 256), 2 * tc)
+        x = jnp.concatenate(
+            [cot[:, pl.ds(start + k * GR, GR), :].reshape(hg, tc) for k in range(2)], axis=1)
+        xs[:, lanes] = x
+        ghs[:, lanes] = dotf(k2[...], x)
+        y = dotf(x, es[1]).reshape(heads, GR, 8 * ch)
+        y = jnp.sum(jnp.where(iota((heads, 1, 8 * ch), 0) == lane_c, y, 0.0), axis=0)
+        rs[pl.ds(start, GR), :] = y[:, : 4 * ch]
+        rs[pl.ds(start + GR, GR), :] = y[:, 4 * ch :]
+        y = dotf(ecx[...], x)
+        cs[...] += y[:, :tc] + y[:, tc:]
+        return carry
+
+    lax.fori_loop(0, groups // 2, ahead, 0)
+
     for inside, own, copies, keep in segments:
 
         @pl.when(own)
@@ -172,41 +203,35 @@
     ns[: 2 * ch, :] = jnp.ones((2 * ch, tc), BF)
     ns[2 * ch : 4 * ch, :] = jnp.where(
         edge(col_first, col_last, iota((2 * ch, tc), 1), tc), 1.0, 0.0).astype(BF)
-    cs[...] = jnp.zeros_like(cs)
 
     chunk = 128
-    lane_c = iota((1, 1, 4 * ch), 2) % ch
+    n = chunk // GR
 
     def group(g, carry):
-        start = pl.multiple_of(g * GR, GR)
-        lanes = pl.ds(pl.multiple_of(g * tc, 128), tc)
-        x = cot[:, pl.ds(start, GR), :].reshape(hg, tc)
-        xs[:, lanes] = x
-        q = qs[pl.ds(start, GR), :]
-        total = jnp.zeros((GR, 4 * ch), F32)
+        start = pl.multiple_of(g * 2 * GR, 2 * GR)
+        q = [qs[pl.ds(start + j * GR, GR), :] for j in range(2)]
+        total = jnp.zeros((GR, 8 * ch), F32)
         for k in range(cg // chunk):
             rows = slice(k * chunk, (k + 1) * chunk)
-            n = chunk // GR
-            m = (cm[rows, :].reshape(n, GR, 8 * ch) * q[None]).reshape(chunk, 8 * ch)
-            u = dotf(m, ns[...])
-            gh = dotf(k2[rows, :], x)
-            t = jnp.tanh(u)
-            p = 1.0 + t
-            h = u * p
-            gc = (gh * (p + h - h * t)).astype(BF)
-            hid[rows, lanes] = h.astype(BF)
-            gcs[rows, :] = gc
-            y = dotf(gc, es[0]).reshape(n, GR, 4 * ch)
-            pick = iota((n, 1, 4 * ch), 0) + k * n == lane_c
-            total = total + jnp.sum(jnp.where(pick, y, 0.0), axis=0)
-        y = dotf(x, es[1]).reshape(heads, GR, 4 * ch)
-        total = total + jnp.sum(jnp.where(iota((heads, 1, 4 * ch), 0) == lane_c, y, 0.0), axis=0)
-        rs[pl.ds(start, GR), :] = total
-        kind = (g + groups - 1) // groups + g // (groups - 1)
-        cs[...] += dotf(ecol[kind], gcs[...]) + dotf(ecx[...], x)
+            mask = cm[rows, :].reshape(n, GR, 8 * ch)
+            for j in range(2):
+                lanes = pl.ds(pl.multiple_of(g * 2 * tc + j * tc, 128), tc)
+                u = dotf((mask * q[j][None]).reshape(chunk, 8 * ch), ns[...])
+                t = jnp.tanh(u)
+                p = 1.0 + t
+                h = u * p
+                hid[rows, lanes] = h.astype(BF)
+                gcs[rows, j * tc : (j + 1) * tc] = (ghs[rows, lanes] * (p + h - h * t)).astype(BF)
+            y = dotf(gcs[rows, :], es[0]).reshape(n, GR, 8 * ch)
+            total = total + jnp.sum(jnp.where(iota((n, 1, 8 * ch), 0) + k * n == lane_c, y, 0.0), axis=0)
+        rs[pl.ds(start, GR), :] += total[:, : 4 * ch]
+        rs[pl.ds(start + GR, GR), :] += total[:, 4 * ch :]
+        first = (g + groups - 1) // groups
+        last = g // (groups // 2 - 1) + 1
+        cs[...] += dotf(ecol[first], gcs[:, :tc]) + dotf(ecol[last], gcs[:, tc:])
         return carry
 
-    lax.fori_loop(0, groups, group, 0)
+    lax.fori_loop(0, groups // 2, group, 0)
 
     prod = dotf(hid[...], xs[...], ((1,), (1,)))
     prod = jnp.sum(jnp.where(same, prod, 0.0).reshape(ch, GR, hg), axis=1)
@@ -226,7 +251,7 @@
     small[ch + 8 :, :] = jnp.zeros((ch - 8, 4 * ch), F32)
 
     eye = iota((ch, ch), 0) == iota((ch, ch), 1)
-    whs = scale * dotf(jnp.where(iota((ch, heads), 0) == iota((ch, heads), 1), 1.0, 0.0).astype(BF), wh[...], ((1,), (1,)))
+    whs = scale * jnp.concatenate([wh[...].astype(F32), jnp.zeros((ch - heads, ch), F32)], axis=0)
     zc = jnp.zeros((ch, ch), F32)
 
     def spread(tap):
@@ -351,7 +376,7 @@
     p3r = (gwsend, gwrecv, r3s, r3r)
     s3r = to_row(*p3r)
     start(s3r)
-    gf_out[...] = (dotf(glb, wl[...], ((1,), (1,))) + dotf(grb, wr[...], ((1,), (1,)))).astype(BF)
+    gf_out[...] = (dotf(glb, wl[...]) + dotf(grb, wr[...])).astype(BF)
     arrived(from_col(*p3c))
     sent(s3c)
     sent(s2r)
@@ -362,14 +387,13 @@
             gk_out[3 * a + b : 3 * a + b + 1, :] = scale * (
                 full[ch + a : ch + a + 1, b * ch : (b + 1) * ch]
                 + full[ch + 3 + b : ch + 4 + b, a * ch : (a + 1) * ch])
-    gp_out[...] = scale * scale * dotf(hc, wh[...].astype(F32), ((1,), (1,)), HI)
-    gh_out[...] = scale * (pc + dotf(wp[...].astype(F32), hc, ((0,), (0,)), HI))
+    gp_out[...] = scale * scale * dotf(hc, wh[...].astype(F32), precision=HI)
+    gh_out[...] = (scale * (pc + dotf(wp[...].astype(F32), hc, ((0,), (0,)), HI))).T
     arrived(from_row(*p3r))
     for m in row_mates:
         part = part + gwrecv[m].astype(F32)
-    part = part.T
-    gwl_out[...] = part[:, :ch]
-    gwr_out[...] = part[:, ch:]
+    gwl_out[...] = part[:ch]
+    gwr_out[...] = part[ch:]
     sent(s3r)
 
 
@@ -384,19 +408,23 @@
     ag = -(-(pp + 4 + pr) // 16) * 16
     vm = pl.BlockSpec(memory_space=pltpu.VMEM)
     dma = pltpu.SemaphoreType.DMA
-    return pl.pallas_call(
+    operands = (bin_features, w_left.T, w_right.T, depth_kernel, w_point, w_head.T, cotangent)
+    gf, gwl, gwr, gk, gp, gh = pl.pallas_call(
         functools.partial(tile_kernel, scale),
         out_shape=(
             jax.ShapeDtypeStruct((tr, d), BF),
-            jax.ShapeDtypeStruct((d, ch), F32),
-            jax.ShapeDtypeStruct((d, ch), F32),
+            jax.ShapeDtypeStruct((ch, d), F32),
+            jax.ShapeDtypeStruct((ch, d), F32),
             jax.ShapeDtypeStruct((9, ch), F32),
             jax.ShapeDtypeStruct((ch, ch), F32),
-            jax.ShapeDtypeStruct((ch, heads), F32),
+            jax.ShapeDtypeStruct((heads, ch), F32),
         ),
-        in_specs=[vm] * 7,
+        in_specs=[pl.BlockSpec(memory_space=pltpu.HBM)] * 7,
         out_specs=(vm,) * 6,
         scratch_shapes=[
+            *(pltpu.VMEM(v.shape, v.dtype) for v in operands),
+            dma((7,)),
+            pltpu.VMEM((cg, groups * tc), F32),
             pltpu.VMEM((tr + 32, ch), F32),
             pltpu.VMEM((tc + 32, ch), F32),
             pltpu.VMEM((tr + 16, ch), F32),
@@ -406,12 +434,12 @@
             pltpu.VMEM((8 * ch, tc), BF),
             pltpu.VMEM((cg, hg), BF),
             pltpu.VMEM((cg, 8 * ch), BF),
-            pltpu.VMEM((2, tc, 4 * ch), BF),
+            pltpu.VMEM((2, 2 * tc, 8 * ch), BF),
             pltpu.VMEM((3, 4 * ch, cg), BF),
             pltpu.VMEM((4 * ch, hg), BF),
             pltpu.VMEM((tr, 4 * ch), F32),
             pltpu.VMEM((4 * ch, tc), F32),
-            pltpu.VMEM((cg, tc), BF),
+            pltpu.VMEM((cg, 2 * tc), BF),
             pltpu.VMEM((cg, groups * tc), BF),
             pltpu.VMEM((hg, groups * tc), BF),
             pltpu.VMEM((tr + 32, 4 * ch), F32),
@@ -440,8 +468,9 @@
             dma((3,)),
         ],
         compiler_params=pltpu.CompilerParams(
-            vmem_limit_bytes=48 * 1024 * 1024, collective_id=0, has_side_effects=True),
-    )(bin_features, w_left, w_right, depth_kernel, w_point, w_head, cotangent)
+            vmem_limit_bytes=63 * 1024 * 1024, collective_id=0, has_side_effects=True),
+    )(*operands)
+    return gf, gwl.T, gwr.T, gk, gp, gh.T
 
 
 def solution(mesh):

time: 51.9 us -> 44 us (0.85)
  Pallas kernels: 40.5 us -> 34.5 us
  local copies, waits for them, and re-layouts: 10.3 us -> 8.54 us
    pallas_call x1, Pallas kernels: 40.5 us -> 34.5 us  [body(): pl.pallas_call(functools.partial(tile_kernel, scale), out_shape=(jax.Shap...]
    pallas_call x3 -> x0, local copies, waits for them, and re-layouts: 2.15 us -> none  [body(): pl.pallas_call(functools.partial(tile_kernel, scale), out_shape=(jax.Shap...]
    unnamed x14 -> x6, local copies, waits for them, and re-layouts: 8.19 us -> 8.54 us
where the time goes in v3:
time: 44 us; the launch traced here: 43.6 us
  Pallas kernels  34.5 us (78%)
  local copies, waits for them, and re-layouts  8.54 us (19%)
  between operations  0.64 us (1%)
    pallas_call x1, Pallas kernels, body(): pl.pallas_call(functools.partial(tile_kernel, scale), out_shape=(jax.Shap...  34.5 us
    unnamed x6, local copies, waits for them, and re-layouts  8.54 us

profile of v3, /device:TPU:0, one launch (start us, length us, event | category | flops | bytes accessed | tf_op | source)
XLA Modules:
  0.0 43.6 jit_solution(3981584726492625565)
XLA Ops:
  0.6 34.5 %shard_map.118 = (bf16[256,512]{1,0:T(8,128)(2,1)}, f32[32,512]{1,0:T(8,128)}, f32[32,512]{1,0:T(8,128)}, f32[9,32]{1,0:T(8,128)}, f32[32,32]{1,0:T(8,128)}, /*index=5*/f32[24,32]{1,0:T(8,128)}) custom-call(bf16[256,512]{1,0:T(8,128)(2,1)} %feats_hbm.1, bf16[32,512]{1,0:T(8,128)(2,1)} %bitcast.8, bf16[32,512]{1,0:T(8,128)(2,1)} %bitcast.9, f32[9,32]{1,0:T(8,128)} %dk_hbm.1, ...), custom_call_target="tpu_custom_call" | custom-call | tf_op jit(solution)/shard_map/pallas_call | solution.py:412
  35.1 1.7 %copy.19 = bf16[256,512]{1,0:T(8,128)(2,1)} copy(bf16[256,512]{1,0:T(8,128)(2,1)} %get-tuple-element.24) | data formatting | bytes 524288
  36.8 1.5 %copy.20 = f32[512,32]{0,1:T(8,128)} copy(f32[512,32]{0,1:T(8,128)} %bitcast.7) | data formatting | bytes 131072
  38.2 1.5 %copy.21 = f32[512,32]{0,1:T(8,128)} copy(f32[512,32]{0,1:T(8,128)} %bitcast.6) | data formatting | bytes 131072
  39.7 1.3 %copy.22 = f32[9,32]{1,0:T(8,128)} copy(f32[9,32]{1,0:T(8,128)} %get-tuple-element.27) | data formatting | bytes 2304
  41.0 1.3 %copy.23 = f32[32,32]{1,0:T(8,128)} copy(f32[32,32]{1,0:T(8,128)} %get-tuple-element.28) | data formatting | bytes 8192
  42.3 1.3 %copy.24 = f32[32,24]{0,1:T(8,128)} copy(f32[32,24]{0,1:T(8,128)} %bitcast.10) | data formatting | bytes 6144

commit v4 on v3

--- a/solution.py
+++ b/solution.py
@@ -46,6 +46,7 @@
                 feats, wl, wr, dk, wp, wh, cot, load_sem, ghs,
                 lext, rext, plx, prx, small, qs, ns, k2, cm, es, ecol, ecx, rs, cs, gcs, hid, xs, zl, zr,
                 proj, lbuf, rbuf, colsend, colrecv, rowsend, rowrecv, halosend, halorecv,
+                smsend, smrecv, m1s, m1r,
                 agsend, agrecv, spsend, sprecv, sfin, gwsend, gwrecv, window,
                 rseg_send, rseg_recv, lseg_send, lseg_recv, c1s, c1r, r1s, r1r, h1s, h1r,
                 c2s, c2r, r2s, r2r, c3s, c3r, r3s, r3r, local_sem):
@@ -233,23 +234,8 @@
 
     lax.fori_loop(0, groups // 2, group, 0)
 
-    prod = dotf(hid[...], xs[...], ((1,), (1,)))
-    prod = jnp.sum(jnp.where(same, prod, 0.0).reshape(ch, GR, hg), axis=1)
-    e_h = jnp.where(iota((hg, ch), 0) // GR == iota((hg, ch), 1), 1.0, 0.0)
-    hc = dotf(prod, e_h, precision=HI)
     cst = cs[...].T
     rsv = rs[...]
-    pc = dotf(l_sh[1], rsv[:, 3 * ch :], ((0,), (0,)), HI) + dotf(r_sh[1], cst[:, 3 * ch :], ((0,), (0,)), HI)
-    small[:ch, :] = jnp.concatenate([hc, pc, jnp.zeros((ch, 2 * ch), F32)], axis=1)
-    rows_out = []
-    zero_l, zero_r = jnp.zeros((tr, ch), F32), jnp.zeros((tc, ch), F32)
-    for a in range(3):
-        rows_out.append(jnp.sum(jnp.concatenate([l_sh[a]] * 3 + [zero_l], axis=1) * rsv, axis=0, keepdims=True))
-    for b in range(3):
-        rows_out.append(jnp.sum(jnp.concatenate([r_sh[b]] * 3 + [zero_r], axis=1) * cst, axis=0, keepdims=True))
-    small[ch : ch + 8, :] = jnp.concatenate(rows_out + [jnp.zeros((2, 4 * ch), F32)], axis=0)
-    small[ch + 8 :, :] = jnp.zeros((ch - 8, 4 * ch), F32)
-
     eye = iota((ch, ch), 0) == iota((ch, ch), 1)
     whs = scale * jnp.concatenate([wh[...].astype(F32), jnp.zeros((ch - heads, ch), F32)], axis=0)
     zc = jnp.zeros((ch, ch), F32)
@@ -273,8 +259,7 @@
 
     lanes = 4 * ch
     pp, sp = tr // 4 // n_col, 2 * ch // n_col
-    colsend[:, :pp, :] = pack(plx[8 : 8 + tr, :]).reshape(n_col, pp, lanes)
-    colsend[:, pp:, :] = small[...].reshape(n_col, sp, lanes)
+    colsend[...] = pack(plx[8 : 8 + tr, :]).reshape(n_col, pp, lanes)
     pad = jnp.zeros((8, 3 * ch), F32)
     halosend[0] = jnp.concatenate([plx[:8, :], pad], axis=1)
     halosend[1] = jnp.concatenate([plx[8 + tr :, :], pad], axis=1)
@@ -314,14 +299,28 @@
     start(s1r)
     pl.when(row > 0)(hup.start)
     pl.when(row < n_row - 1)(hdown.start)
+    prod = dotf(hid[...], xs[...], ((1,), (1,)))
+    prod = jnp.sum(jnp.where(same, prod, 0.0).reshape(ch, GR, hg), axis=1)
+    e_h = jnp.where(iota((hg, ch), 0) // GR == iota((hg, ch), 1), 1.0, 0.0)
+    hc = dotf(prod, e_h, precision=HI)
+    pc = dotf(l_sh[1], rsv[:, 3 * ch :], ((0,), (0,)), HI) + dotf(r_sh[1], cst[:, 3 * ch :], ((0,), (0,)), HI)
+    small[:ch, :] = jnp.concatenate([hc, pc, jnp.zeros((ch, 2 * ch), F32)], axis=1)
+    rows_out = []
+    zero_l, zero_r = jnp.zeros((tr, ch), F32), jnp.zeros((tc, ch), F32)
+    for a in range(3):
+        rows_out.append(jnp.sum(jnp.concatenate([l_sh[a]] * 3 + [zero_l], axis=1) * rsv, axis=0, keepdims=True))
+    for b in range(3):
+        rows_out.append(jnp.sum(jnp.concatenate([r_sh[b]] * 3 + [zero_r], axis=1) * cst, axis=0, keepdims=True))
+    small[ch : ch + 8, :] = jnp.concatenate(rows_out + [jnp.zeros((2, 4 * ch), F32)], axis=0)
+    small[ch + 8 :, :] = jnp.zeros((ch - 8, 4 * ch), F32)
+    smsend[...] = small[...].reshape(n_col, sp, lanes)
+    p1s = (lambda m: smsend.at[m], smrecv, m1s, m1r)
+    s1s = to_col(*p1s)
+    start(s1s)
     arrived(from_col(*p1c))
     piece = colsend[col]
     for m in col_mates:
         piece = piece + colrecv[m]
-    spsend[...] = piece[pp:]
-    p2r = (spsend, sprecv, r2s, r2r)
-    s2r = to_row(*p2r)
-    start(s2r)
     arrived(from_row(*p1r))
     right = rowsend[...]
     for m in row_mates:
@@ -339,20 +338,21 @@
 
     fill = [jnp.zeros((agsend.shape[0] - pp - 4 - pr, lanes), F32)] if agsend.shape[0] > pp + 4 + pr else []
     agsend[...] = jnp.concatenate(
-        [right, pack(halorecv[0, :, :ch]), pack(halorecv[1, :, :ch]), piece[:pp]] + fill, axis=0).astype(BF)
+        [right, pack(halorecv[0, :, :ch]), pack(halorecv[1, :, :ch]), piece] + fill, axis=0).astype(BF)
     p2c = (lambda m: agsend, agrecv, c2s, c2r)
     s2c = to_col(*p2c)
     start(s2c)
+    arrived(from_col(*p1s))
+    part = smsend[col]
+    for m in col_mates:
+        part = part + smrecv[m]
+    spsend[...] = part
+    p2r = (spsend, sprecv, r2s, r2r)
+    s2r = to_row(*p2r)
+    start(s2r)
     sent(s1c)
     sent(s1r)
-    arrived(from_row(*p2r))
-    total = spsend[...]
-    for m in row_mates:
-        total = total + sprecv[m]
-    sfin[col] = total
-    p3c = (lambda m: sfin.at[col], sfin, c3s, c3r)
-    s3c = to_col(*p3c)
-    start(s3c)
+    sent(s1s)
     arrived(from_col(*p2c))
     sent(s2c)
     agrecv[col] = agsend[...]
@@ -376,6 +376,14 @@
     p3r = (gwsend, gwrecv, r3s, r3r)
     s3r = to_row(*p3r)
     start(s3r)
+    arrived(from_row(*p2r))
+    total = spsend[...]
+    for m in row_mates:
+        total = total + sprecv[m]
+    sfin[col] = total
+    p3c = (lambda m: sfin.at[col], sfin, c3s, c3r)
+    s3c = to_col(*p3c)
+    start(s3c)
     gf_out[...] = (dotf(glb, wl[...]) + dotf(grb, wr[...])).astype(BF)
     arrived(from_col(*p3c))
     sent(s3c)
@@ -397,6 +405,16 @@
     sent(s3r)
 
 
+def move_kernel(*refs):
+    sems = refs[-1]
+    n = len(refs) // 2
+    copies = [pltpu.make_async_copy(refs[k], refs[n + k], sems.at[k]) for k in range(n)]
+    for c in copies:
+        c.start()
+    for c in copies:
+        c.wait()
+
+
 def body(bin_features, w_left, w_right, depth_kernel, w_point, w_head, cotangent):
     ch, heads = w_head.shape
     tr, tc = cotangent.shape[1:]
@@ -409,15 +427,15 @@
     vm = pl.BlockSpec(memory_space=pltpu.VMEM)
     dma = pltpu.SemaphoreType.DMA
     operands = (bin_features, w_left.T, w_right.T, depth_kernel, w_point, w_head.T, cotangent)
-    gf, gwl, gwr, gk, gp, gh = pl.pallas_call(
+    outs = pl.pallas_call(
         functools.partial(tile_kernel, scale),
         out_shape=(
-            jax.ShapeDtypeStruct((tr, d), BF),
-            jax.ShapeDtypeStruct((ch, d), F32),
-            jax.ShapeDtypeStruct((ch, d), F32),
-            jax.ShapeDtypeStruct((9, ch), F32),
-            jax.ShapeDtypeStruct((ch, ch), F32),
-            jax.ShapeDtypeStruct((heads, ch), F32),
+            pltpu.VMEM((tr, d), BF),
+            pltpu.VMEM((ch, d), F32),
+            pltpu.VMEM((ch, d), F32),
+            pltpu.VMEM((9, ch), F32),
+            pltpu.VMEM((ch, ch), F32),
+            pltpu.VMEM((heads, ch), F32),
         ),
         in_specs=[pl.BlockSpec(memory_space=pltpu.HBM)] * 7,
         out_specs=(vm,) * 6,
@@ -447,12 +465,15 @@
             pltpu.VMEM((tr, lanes), BF),
             pltpu.VMEM((2, 16, lanes), BF),
             pltpu.VMEM((tc + 32, lanes), BF),
-            pltpu.VMEM((n_col, pp + sp, lanes), F32),
-            pltpu.VMEM((n_col, pp + sp, lanes), F32),
+            pltpu.VMEM((n_col, pp, lanes), F32),
+            pltpu.VMEM((n_col, pp, lanes), F32),
             pltpu.VMEM((pr, lanes), F32),
             pltpu.VMEM((n_row, pr, lanes), F32),
             pltpu.VMEM((2, 8, lanes), F32),
             pltpu.VMEM((2, 8, lanes), F32),
+            pltpu.VMEM((n_col, sp, lanes), F32),
+            pltpu.VMEM((n_col, sp, lanes), F32),
+            dma((n_col,)), dma((n_col,)),
             pltpu.VMEM((ag, lanes), BF),
             pltpu.VMEM((n_col, ag, lanes), BF),
             pltpu.VMEM((sp, lanes), F32),
@@ -470,6 +491,15 @@
         compiler_params=pltpu.CompilerParams(
             vmem_limit_bytes=63 * 1024 * 1024, collective_id=0, has_side_effects=True),
     )(*operands)
+    hbm = pl.BlockSpec(memory_space=pltpu.HBM)
+    gf, gwl, gwr, gk, gp, gh = pl.pallas_call(
+        move_kernel,
+        out_shape=tuple(jax.ShapeDtypeStruct(v.shape, v.dtype) for v in outs),
+        in_specs=[vm] * 6,
+        out_specs=(hbm,) * 6,
+        scratch_shapes=[dma((6,))],
+        compiler_params=pltpu.CompilerParams(vmem_limit_bytes=16 * 1024 * 1024),
+    )(*outs)
     return gf, gwl.T, gwr.T, gk, gp, gh.T
 
 

time: 44 us -> 33.8 us (0.77)
  local copies, waits for them, and re-layouts: 8.54 us -> 0 us
  Pallas kernels: 34.5 us -> 33 us
    unnamed x6 -> x0, local copies, waits for them, and re-layouts: 8.54 us -> none
    pallas_call x1 -> x2, Pallas kernels: 34.5 us -> 33 us  [the longest x1 32.2 us: body(): pl.pallas_call(functools.partial(tile_kernel, scale), out_shape=(pltpu.VM...]
where the time goes in v4:
time: 33.8 us; the launch traced here: 33.6 us
  Pallas kernels  33 us (98%)
  between operations  0.64 us (2%)
    pallas_call x1, Pallas kernels, body(): pl.pallas_call(functools.partial(tile_kernel, scale), out_shape=(pltpu.VM...  32.2 us
    pallas_call x1, Pallas kernels, body(): pl.pallas_call(move_kernel, out_shape=tuple((jax.ShapeDtypeStruct(v.shape...  0.8 us

profile of v4, /device:TPU:0, one launch (start us, length us, event | category | flops | bytes accessed | tf_op | source)
XLA Modules:
  0.0 33.6 jit_solution(10948676355746523195)
XLA Ops:
  0.6 32.2 %shard_map.118 = (bf16[256,512]{1,0:T(8,128)(2,1)S(1)}, f32[32,512]{1,0:T(8,128)S(1)}, f32[32,512]{1,0:T(8,128)S(1)}, f32[9,32]{1,0:T(8,128)S(1)}, f32[32,32]{1,0:T(8,128)S(1)}, /*index=5*/f32[24,32]{1,0:T(8,128)S(1)}) custom-call(bf16[256,512]{1,0:T(8,128)(2,1)} %feats_hbm.1, bf16[32,512]{1,0:T(8,128)(2,1)} %bitcast.6, bf16[32,512]{1,0:T(8,128)(2,1)} %bitcast.7, ...), custom_call_target="tpu_custom_call" | custom-call | tf_op jit(solution)/shard_map/pallas_call | solution.py:430
  32.8 0.8 %shard_map.119 = (bf16[256,512]{1,0:T(8,128)(2,1)}, f32[32,512]{1,0:T(8,128)}, f32[32,512]{1,0:T(8,128)}, f32[9,32]{1,0:T(8,128)}, f32[32,32]{1,0:T(8,128)}, /*index=5*/f32[24,32]{1,0:T(8,128)}) custom-call(bf16[256,512]{1,0:T(8,128)(2,1)S(1)} %get-tuple-element.18.refs_0_, f32[32,512]{1,0:T(8,128)S(1)} %get-tuple-element.19.refs_1_, ...), custom_call_target="tpu_custom_call" | custom-call | tf_op jit(solution)/shard_map/pallas_call | solution.py:495

commit v5 on v4

--- a/solution.py
+++ b/solution.py
@@ -44,7 +44,7 @@
 def tile_kernel(scale, feats_hbm, wl_hbm, wr_hbm, dk_hbm, wp_hbm, wh_hbm, cot_hbm,
                 gf_out, gwl_out, gwr_out, gk_out, gp_out, gh_out,
                 feats, wl, wr, dk, wp, wh, cot, load_sem, ghs,
-                lext, rext, plx, prx, small, qs, ns, k2, cm, es, ecol, ecx, rs, cs, gcs, hid, xs, zl, zr,
+                lext, rext, plx, prx, small, qs, ns, k2, cm, es, ecol, colsum, us, fall, fsend, frecv, rs, cs, gcs, hid, xs, zl, zr,
                 proj, lbuf, rbuf, colsend, colrecv, rowsend, rowrecv, halosend, halorecv,
                 smsend, smrecv, m1s, m1r,
                 agsend, agrecv, spsend, sprecv, sfin, gwsend, gwrecv, window,
@@ -121,7 +121,8 @@
     e_c = jnp.where(iota((heads, hg), 1) // GR == iota((heads, hg), 0), 1.0, 0.0).astype(BF)
     w2r = dotf(e_r, w2).astype(BF)
     same = iota((cg, hg), 0) % GR == iota((cg, hg), 1) % GR
-    k2[...] = jnp.where(same, dotf(w2r, e_c), 0.0).astype(BF)
+    k2[:cg, :] = jnp.where(same, dotf(w2r, e_c), 0.0).astype(BF)
+    k2[cg:, :] = jnp.where(iota((ch, hg), 0) == iota((ch, hg), 1) // GR, 1.0, 0.0).astype(BF)
 
     jj, part = iota((2 * tc, 8 * ch), 0), iota((2 * tc, 8 * ch), 1)
     paired = jj // tc == part // (4 * ch)
@@ -129,15 +130,13 @@
     drop = ((part == 0) & (jj < STEP) & col_first) | ((part == 2) & (jj >= tc - STEP) & col_last)
     es[0] = jnp.where(paired & ~drop & (part != 3), 1.0, 0.0).astype(BF)
     es[1] = jnp.where(paired & (part == 3), 1.0, 0.0).astype(BF)
-    pr, ci = iota((4 * ch, cg), 0), iota((4 * ch, cg), 1)
-    mine = (pr % ch == ci // GR) & (pr // ch < 3)
-    top = (pr // ch == 0) & (ci % GR < STEP) & row_first
-    low = (pr // ch == 2) & (ci % GR >= GR - STEP) & row_last
-    ecol[0] = jnp.where(mine & ~top, 1.0, 0.0).astype(BF)
-    ecol[1] = jnp.where(mine, 1.0, 0.0).astype(BF)
-    ecol[2] = jnp.where(mine & ~low, 1.0, 0.0).astype(BF)
-    ecx[...] = jnp.where(
-        iota((4 * ch, hg), 0) == 3 * ch + iota((4 * ch, hg), 1) // GR, 1.0, 0.0).astype(BF)
+    pr, ci = iota((ch, cg), 0), iota((ch, cg), 1)
+    mine = pr == ci // GR
+    ecol[0] = jnp.where(mine & (ci % GR < STEP) & row_first, 1.0, 0.0).astype(BF)
+    ecol[1] = jnp.where(mine & (ci % GR >= GR - STEP) & row_last, 1.0, 0.0).astype(BF)
+    colsum[...] = jnp.zeros_like(colsum)
+    fs = [remote(feats, fall.at[row], fsend.at[m], frecv.at[row], (m, col)) for m in row_mates]
+    fr = [remote(feats, fall.at[m], fsend.at[m], frecv.at[m], (m, col)) for m in row_mates]
     cs[...] = jnp.zeros_like(cs)
     lane_c = iota((1, 1, 8 * ch), 2) % ch
     loads[6].wait()
@@ -148,13 +147,13 @@
         x = jnp.concatenate(
             [cot[:, pl.ds(start + k * GR, GR), :].reshape(hg, tc) for k in range(2)], axis=1)
         xs[:, lanes] = x
-        ghs[:, lanes] = dotf(k2[...], x)
+        w = dotf(k2[...], x)
+        ghs[:, lanes] = w[:cg]
+        cs[...] += w[cg:, :tc] + w[cg:, tc:]
         y = dotf(x, es[1]).reshape(heads, GR, 8 * ch)
         y = jnp.sum(jnp.where(iota((heads, 1, 8 * ch), 0) == lane_c, y, 0.0), axis=0)
         rs[pl.ds(start, GR), :] = y[:, : 4 * ch]
         rs[pl.ds(start + GR, GR), :] = y[:, 4 * ch :]
-        y = dotf(ecx[...], x)
-        cs[...] += y[:, :tc] + y[:, tc:]
         return carry
 
     lax.fori_loop(0, groups // 2, ahead, 0)
@@ -181,6 +180,8 @@
         down.wait_send()
         up.wait_recv()
 
+    for copy in fs:
+        copy.start()
     lext[0:16, :] = lbuf[0, :, :ch].astype(F32)
     lext[16 : 16 + tr, :] = proj[:, :ch].astype(F32)
     lext[16 + tr :, :] = lbuf[1, :, :ch].astype(F32)
@@ -205,36 +206,42 @@
     ns[2 * ch : 4 * ch, :] = jnp.where(
         edge(col_first, col_last, iota((2 * ch, tc), 1), tc), 1.0, 0.0).astype(BF)
 
-    chunk = 128
+    chunk = 64
     n = chunk // GR
 
-    def group(g, carry):
+    def pair(g, slot):
         start = pl.multiple_of(g * 2 * GR, 2 * GR)
-        q = [qs[pl.ds(start + j * GR, GR), :] for j in range(2)]
-        total = jnp.zeros((GR, 8 * ch), F32)
+        mask = cm[...].reshape(ch, GR, 8 * ch)
+        for j in range(2):
+            q = qs[pl.ds(start + j * GR, GR), :]
+            us[slot, :, j * tc : (j + 1) * tc] = dotf((mask * q[None]).reshape(cg, 8 * ch), ns[...])
+        lanes = pl.ds(pl.multiple_of(g * 2 * tc, 256), 2 * tc)
         for k in range(cg // chunk):
             rows = slice(k * chunk, (k + 1) * chunk)
-            mask = cm[rows, :].reshape(n, GR, 8 * ch)
-            for j in range(2):
-                lanes = pl.ds(pl.multiple_of(g * 2 * tc + j * tc, 128), tc)
-                u = dotf((mask * q[j][None]).reshape(chunk, 8 * ch), ns[...])
-                t = jnp.tanh(u)
-                p = 1.0 + t
-                h = u * p
-                hid[rows, lanes] = h.astype(BF)
-                gcs[rows, j * tc : (j + 1) * tc] = (ghs[rows, lanes] * (p + h - h * t)).astype(BF)
-            y = dotf(gcs[rows, :], es[0]).reshape(n, GR, 8 * ch)
-            total = total + jnp.sum(jnp.where(iota((n, 1, 8 * ch), 0) + k * n == lane_c, y, 0.0), axis=0)
+            u = us[slot, rows, :]
+            t = jnp.tanh(u)
+            p = 1.0 + t
+            h = u * p
+            hid[rows, lanes] = h.astype(BF)
+            gc = ghs[rows, lanes] * (p + h - h * t)
+            gcs[rows, lanes] = gc.astype(BF)
+            colsum[k * n : (k + 1) * n] += jnp.sum(gc.reshape(n, 2, 8, 2 * tc), axis=1)
+        y = dotf(gcs[:, lanes], es[0]).reshape(ch, GR, 8 * ch)
+        total = jnp.sum(jnp.where(iota((ch, 1, 8 * ch), 0) == lane_c, y, 0.0), axis=0)
         rs[pl.ds(start, GR), :] += total[:, : 4 * ch]
         rs[pl.ds(start + GR, GR), :] += total[:, 4 * ch :]
-        first = (g + groups - 1) // groups
-        last = g // (groups // 2 - 1) + 1
-        cs[...] += dotf(ecol[first], gcs[:, :tc]) + dotf(ecol[last], gcs[:, tc:])
+
+    def group(g, carry):
+        pair(2 * g, 0)
+        pair(2 * g + 1, 1)
         return carry
 
-    lax.fori_loop(0, groups // 2, group, 0)
-
-    cst = cs[...].T
+    lax.fori_loop(0, groups // 4, group, 0)
+    base = jnp.sum(colsum[...], axis=1)
+    base = base[:, :tc] + base[:, tc:]
+    top = dotf(ecol[0], gcs[:, :tc])
+    low = dotf(ecol[1], gcs[:, (groups - 1) * tc :])
+    cst = jnp.concatenate([base - top, base, base - low, cs[...]], axis=0).T
     rsv = rs[...]
     eye = iota((ch, ch), 0) == iota((ch, ch), 1)
     whs = scale * jnp.concatenate([wh[...].astype(F32), jnp.zeros((ch - heads, ch), F32)], axis=0)
@@ -370,12 +377,12 @@
     gr = window[tc + 8 : tc + 8 + tr, :]
     glb, grb = gl.astype(BF), gr.astype(BF)
     both = jnp.concatenate([gl, gr, jnp.zeros((tr, 2 * ch), F32)], axis=1).T[: 2 * ch].astype(BF)
-    part = scale * dotf(both, feats[...])
-
-    gwsend[...] = part.astype(BF)
+
+    gwsend[...] = both
     p3r = (gwsend, gwrecv, r3s, r3r)
     s3r = to_row(*p3r)
     start(s3r)
+    part = dotf(both, feats[...])
     arrived(from_row(*p2r))
     total = spsend[...]
     for m in row_mates:
@@ -398,8 +405,11 @@
     gp_out[...] = scale * scale * dotf(hc, wh[...].astype(F32), precision=HI)
     gh_out[...] = (scale * (pc + dotf(wp[...].astype(F32), hc, ((0,), (0,)), HI))).T
     arrived(from_row(*p3r))
+    arrived(fr)
     for m in row_mates:
-        part = part + gwrecv[m].astype(F32)
+        part = part + dotf(gwrecv[m], fall[m])
+    part = scale * part
+    sent(fs)
     gwl_out[...] = part[:ch]
     gwr_out[...] = part[ch:]
     sent(s3r)
@@ -450,14 +460,17 @@
             pltpu.VMEM((2 * ch, lanes), F32),
             pltpu.VMEM((tr, 8 * ch), BF),
             pltpu.VMEM((8 * ch, tc), BF),
-            pltpu.VMEM((cg, hg), BF),
+            pltpu.VMEM((cg + ch, hg), BF),
             pltpu.VMEM((cg, 8 * ch), BF),
             pltpu.VMEM((2, 2 * tc, 8 * ch), BF),
-            pltpu.VMEM((3, 4 * ch, cg), BF),
-            pltpu.VMEM((4 * ch, hg), BF),
+            pltpu.VMEM((2, ch, cg), BF),
+            pltpu.VMEM((ch, 8, 2 * tc), F32),
+            pltpu.VMEM((2, cg, 2 * tc), F32),
+            pltpu.VMEM((n_row, tr, d), BF),
+            dma((n_row,)), dma((n_row,)),
             pltpu.VMEM((tr, 4 * ch), F32),
-            pltpu.VMEM((4 * ch, tc), F32),
-            pltpu.VMEM((cg, 2 * tc), BF),
+            pltpu.VMEM((ch, tc), F32),
+            pltpu.VMEM((cg, groups * tc), BF),
             pltpu.VMEM((cg, groups * tc), BF),
             pltpu.VMEM((hg, groups * tc), BF),
             pltpu.VMEM((tr + 32, 4 * ch), F32),
@@ -479,8 +492,8 @@
             pltpu.VMEM((sp, lanes), F32),
             pltpu.VMEM((n_row, sp, lanes), F32),
             pltpu.VMEM((n_col, sp, lanes), F32),
-            pltpu.VMEM((2 * ch, d), BF),
-            pltpu.VMEM((n_row, 2 * ch, d), BF),
+            pltpu.VMEM((2 * ch, tr), BF),
+            pltpu.VMEM((n_row, 2 * ch, tr), BF),
             pltpu.VMEM((tr + 2 * tc + 16, ch), F32),
             dma((3, n_row)), dma((3,)), dma((2,)), dma((2,)),
             dma((n_col,)), dma((n_col,)), dma((n_row,)), dma((n_row,)), dma((2,)), dma((2,)),

time: 33.8 us -> 35.7 us (1.056)
  Pallas kernels: 33 us -> 34.9 us
    pallas_call x1, Pallas kernels: 32.2 us -> 34.1 us  [body(): pl.pallas_call(functools.partial(tile_kernel, scale), out_shape=(pltpu.VM...]
where the time goes in v5:
time: 35.7 us; the launch traced here: 35.5 us
  Pallas kernels  34.9 us (98%)
  between operations  0.64 us (2%)
    pallas_call x1, Pallas kernels, body(): pl.pallas_call(functools.partial(tile_kernel, scale), out_shape=(pltpu.VM...  34.1 us
    pallas_call x1, Pallas kernels, body(): pl.pallas_call(move_kernel, out_shape=tuple((jax.ShapeDtypeStruct(v.shape...  0.8 us

profile of v5, /device:TPU:0, one launch (start us, length us, event | category | flops | bytes accessed | tf_op | source)
XLA Modules:
  0.0 35.5 jit_solution(7433064992150977831)
XLA Ops:
  0.6 34.1 %shard_map.118 = (bf16[256,512]{1,0:T(8,128)(2,1)S(1)}, f32[32,512]{1,0:T(8,128)S(1)}, f32[32,512]{1,0:T(8,128)S(1)}, f32[9,32]{1,0:T(8,128)S(1)}, f32[32,32]{1,0:T(8,128)S(1)}, /*index=5*/f32[24,32]{1,0:T(8,128)S(1)}) custom-call(bf16[256,512]{1,0:T(8,128)(2,1)} %feats_hbm.1, bf16[32,512]{1,0:T(8,128)(2,1)} %bitcast.6, bf16[32,512]{1,0:T(8,128)(2,1)} %bitcast.7, ...), custom_call_target="tpu_custom_call" | custom-call | tf_op jit(solution)/shard_map/pallas_call | solution.py:440
  34.7 0.8 %shard_map.119 = (bf16[256,512]{1,0:T(8,128)(2,1)}, f32[32,512]{1,0:T(8,128)}, f32[32,512]{1,0:T(8,128)}, f32[9,32]{1,0:T(8,128)}, f32[32,32]{1,0:T(8,128)}, /*index=5*/f32[24,32]{1,0:T(8,128)}) custom-call(bf16[256,512]{1,0:T(8,128)(2,1)S(1)} %get-tuple-element.18.refs_0_, f32[32,512]{1,0:T(8,128)S(1)} %get-tuple-element.19.refs_1_, ...), custom_call_target="tpu_custom_call" | custom-call | tf_op jit(solution)/shard_map/pallas_call | solution.py:508

commit v6 on v5

--- a/solution.py
+++ b/solution.py
@@ -44,7 +44,7 @@
 def tile_kernel(scale, feats_hbm, wl_hbm, wr_hbm, dk_hbm, wp_hbm, wh_hbm, cot_hbm,
                 gf_out, gwl_out, gwr_out, gk_out, gp_out, gh_out,
                 feats, wl, wr, dk, wp, wh, cot, load_sem, ghs,
-                lext, rext, plx, prx, small, qs, ns, k2, cm, es, ecol, colsum, us, fall, fsend, frecv, rs, cs, gcs, hid, xs, zl, zr,
+                lext, rext, plx, prx, small, qs, ns, k2, cm, es, ecol, colsum, us, rs, cs, gcs, hid, xs, zl, zr,
                 proj, lbuf, rbuf, colsend, colrecv, rowsend, rowrecv, halosend, halorecv,
                 smsend, smrecv, m1s, m1r,
                 agsend, agrecv, spsend, sprecv, sfin, gwsend, gwrecv, window,
@@ -135,8 +135,6 @@
     ecol[0] = jnp.where(mine & (ci % GR < STEP) & row_first, 1.0, 0.0).astype(BF)
     ecol[1] = jnp.where(mine & (ci % GR >= GR - STEP) & row_last, 1.0, 0.0).astype(BF)
     colsum[...] = jnp.zeros_like(colsum)
-    fs = [remote(feats, fall.at[row], fsend.at[m], frecv.at[row], (m, col)) for m in row_mates]
-    fr = [remote(feats, fall.at[m], fsend.at[m], frecv.at[m], (m, col)) for m in row_mates]
     cs[...] = jnp.zeros_like(cs)
     lane_c = iota((1, 1, 8 * ch), 2) % ch
     loads[6].wait()
@@ -180,8 +178,6 @@
         down.wait_send()
         up.wait_recv()
 
-    for copy in fs:
-        copy.start()
     lext[0:16, :] = lbuf[0, :, :ch].astype(F32)
     lext[16 : 16 + tr, :] = proj[:, :ch].astype(F32)
     lext[16 + tr :, :] = lbuf[1, :, :ch].astype(F32)
@@ -378,11 +374,11 @@
     glb, grb = gl.astype(BF), gr.astype(BF)
     both = jnp.concatenate([gl, gr, jnp.zeros((tr, 2 * ch), F32)], axis=1).T[: 2 * ch].astype(BF)
 
-    gwsend[...] = both
+    part = scale * dotf(both, feats[...])
+    gwsend[...] = part.astype(BF)
     p3r = (gwsend, gwrecv, r3s, r3r)
     s3r = to_row(*p3r)
     start(s3r)
-    part = dotf(both, feats[...])
     arrived(from_row(*p2r))
     total = spsend[...]
     for m in row_mates:
@@ -405,11 +401,8 @@
     gp_out[...] = scale * scale * dotf(hc, wh[...].astype(F32), precision=HI)
     gh_out[...] = (scale * (pc + dotf(wp[...].astype(F32), hc, ((0,), (0,)), HI))).T
     arrived(from_row(*p3r))
-    arrived(fr)
     for m in row_mates:
-        part = part + dotf(gwrecv[m], fall[m])
-    part = scale * part
-    sent(fs)
+        part = part + gwrecv[m].astype(F32)
     gwl_out[...] = part[:ch]
     gwr_out[...] = part[ch:]
     sent(s3r)
@@ -466,8 +459,6 @@
             pltpu.VMEM((2, ch, cg), BF),
             pltpu.VMEM((ch, 8, 2 * tc), F32),
             pltpu.VMEM((2, cg, 2 * tc), F32),
-            pltpu.VMEM((n_row, tr, d), BF),
-            dma((n_row,)), dma((n_row,)),
             pltpu.VMEM((tr, 4 * ch), F32),
             pltpu.VMEM((ch, tc), F32),
             pltpu.VMEM((cg, groups * tc), BF),
@@ -492,8 +483,8 @@
             pltpu.VMEM((sp, lanes), F32),
             pltpu.VMEM((n_row, sp, lanes), F32),
             pltpu.VMEM((n_col, sp, lanes), F32),
-            pltpu.VMEM((2 * ch, tr), BF),
-            pltpu.VMEM((n_row, 2 * ch, tr), BF),
+            pltpu.VMEM((2 * ch, d), BF),
+            pltpu.VMEM((n_row, 2 * ch, d), BF),
             pltpu.VMEM((tr + 2 * tc + 16, ch), F32),
             dma((3, n_row)), dma((3,)), dma((2,)), dma((2,)),
             dma((n_col,)), dma((n_col,)), dma((n_row,)), dma((n_row,)), dma((2,)), dma((2,)),

time: 35.7 us -> 29.1 us (0.82)
  Pallas kernels: 34.9 us -> 28.3 us
    pallas_call x1, Pallas kernels: 34.1 us -> 27.5 us  [body(): pl.pallas_call(functools.partial(tile_kernel, scale), out_shape=(pltpu.VM...]
where the time goes in v6:
time: 29.1 us; the launch traced here: 29 us
  Pallas kernels  28.3 us (97%)
  between operations  0.64 us (2%)
    pallas_call x1, Pallas kernels, body(): pl.pallas_call(functools.partial(tile_kernel, scale), out_shape=(pltpu.VM...  27.5 us
    pallas_call x1, Pallas kernels, body(): pl.pallas_call(move_kernel, out_shape=tuple((jax.ShapeDtypeStruct(v.shape...  0.8 us

profile of v6, /device:TPU:0, one launch (start us, length us, event | category | flops | bytes accessed | tf_op | source)
XLA Modules:
  0.0 29.0 jit_solution(12657586489841142919)
XLA Ops:
  0.6 27.5 %shard_map.118 = (bf16[256,512]{1,0:T(8,128)(2,1)S(1)}, f32[32,512]{1,0:T(8,128)S(1)}, f32[32,512]{1,0:T(8,128)S(1)}, f32[9,32]{1,0:T(8,128)S(1)}, f32[32,32]{1,0:T(8,128)S(1)}, /*index=5*/f32[24,32]{1,0:T(8,128)S(1)}) custom-call(bf16[256,512]{1,0:T(8,128)(2,1)} %feats_hbm.1, bf16[32,512]{1,0:T(8,128)(2,1)} %bitcast.6, bf16[32,512]{1,0:T(8,128)(2,1)} %bitcast.7, ...), custom_call_target="tpu_custom_call" | custom-call | tf_op jit(solution)/shard_map/pallas_call | solution.py:433
  28.2 0.8 %shard_map.119 = (bf16[256,512]{1,0:T(8,128)(2,1)}, f32[32,512]{1,0:T(8,128)}, f32[32,512]{1,0:T(8,128)}, f32[9,32]{1,0:T(8,128)}, f32[32,32]{1,0:T(8,128)}, /*index=5*/f32[24,32]{1,0:T(8,128)}) custom-call(bf16[256,512]{1,0:T(8,128)(2,1)S(1)} %get-tuple-element.18.refs_0_, f32[32,512]{1,0:T(8,128)S(1)} %get-tuple-element.19.refs_1_, ...), custom_call_target="tpu_custom_call" | custom-call | tf_op jit(solution)/shard_map/pallas_call | solution.py:499

commit v7 on v6

--- a/solution.py
+++ b/solution.py
@@ -202,7 +202,7 @@
     ns[2 * ch : 4 * ch, :] = jnp.where(
         edge(col_first, col_last, iota((2 * ch, tc), 1), tc), 1.0, 0.0).astype(BF)
 
-    chunk = 64
+    chunk = 32
     n = chunk // GR
 
     def pair(g, slot):

time: 29.1 us -> 29.1 us (level)
  no operation moved by 1% of the time
where the time goes in v7:
time: 29.1 us; the launch traced here: 29 us
  Pallas kernels  28.3 us (97%)
  between operations  0.64 us (2%)
    pallas_call x1, Pallas kernels, body(): pl.pallas_call(functools.partial(tile_kernel, scale), out_shape=(pltpu.VM...  27.5 us
    pallas_call x1, Pallas kernels, body(): pl.pallas_call(move_kernel, out_shape=tuple((jax.ShapeDtypeStruct(v.shape...  0.8 us

profile of v7, /device:TPU:0, one launch (start us, length us, event | category | flops | bytes accessed | tf_op | source)
XLA Modules:
  0.0 29.0 jit_solution(12657586489841142919)
XLA Ops:
  0.6 27.5 %shard_map.118 = (bf16[256,512]{1,0:T(8,128)(2,1)S(1)}, f32[32,512]{1,0:T(8,128)S(1)}, f32[32,512]{1,0:T(8,128)S(1)}, f32[9,32]{1,0:T(8,128)S(1)}, f32[32,32]{1,0:T(8,128)S(1)}, /*index=5*/f32[24,32]{1,0:T(8,128)S(1)}) custom-call(bf16[256,512]{1,0:T(8,128)(2,1)} %feats_hbm.1, bf16[32,512]{1,0:T(8,128)(2,1)} %bitcast.6, bf16[32,512]{1,0:T(8,128)(2,1)} %bitcast.7, ...), custom_call_target="tpu_custom_call" | custom-call | tf_op jit(solution)/shard_map/pallas_call | solution.py:433
  28.2 0.8 %shard_map.119 = (bf16[256,512]{1,0:T(8,128)(2,1)}, f32[32,512]{1,0:T(8,128)}, f32[32,512]{1,0:T(8,128)}, f32[9,32]{1,0:T(8,128)}, f32[32,32]{1,0:T(8,128)}, /*index=5*/f32[24,32]{1,0:T(8,128)}) custom-call(bf16[256,512]{1,0:T(8,128)(2,1)S(1)} %get-tuple-element.18.refs_0_, f32[32,512]{1,0:T(8,128)S(1)} %get-tuple-element.19.refs_1_, ...), custom_call_target="tpu_custom_call" | custom-call | tf_op jit(solution)/shard_map/pallas_call | solution.py:499
